TPU v7x, 128 devices: a whole 4x4x4 slice. The times are simulated.
128 devices in a mesh: gx: 8 (over x, core), gy: 16 (over y, z).
Axes of the slice: x: 4, y: 4, z: 4, core: 2. Of those that a mesh axis runs over, the one named last changes fastest.
Arguments:
- fine_in: bfloat16 [8192, 64, 512], P(('gx', 'gy')), may hold values from -10 to 10
- neighbours: int32 [8192, 6], P(('gx', 'gy')), may hold values from -1 to 8191, as said below
- parent_dev: int32 [8192, 1], P(('gx', 'gy')), may hold values from 0 to 127; in each aligned block of 64 rows (0 to 63, 64 to 127, ...) at most 2 rows name the same one
- parent_cell: int32 [8192], P(('gx', 'gy')), may hold values from 0 to 127
- timestep: int32 [1], replicated, may hold values from 0 to 999
- conv_weight: bfloat16 [7, 64, 64], replicated, may hold values from -0.25 to 0.25
- time_weight: float32 [64, 64], replicated, may hold values from -0.75 to 0.75
- up_weight: bfloat16 [64, 256], replicated, may hold values from -0.75 to 0.75
- coarse_in: bfloat16 [128, 128, 256], P('gx', 'gy'), may hold values from -6 to 6
- coarse_kernel: bfloat16 [9, 256, 256], replicated, may hold values from -0.125 to 0.125
- out_weight: bfloat16 [256, 256], replicated, may hold values from -0.375 to 0.375
- coarse_cot: bfloat16 [128, 128, 256], P('gx', 'gy'), may hold values from -6 to 6
Outputs:
- fine_act: bfloat16 [8192, 64, 512], P(('gx', 'gy'))
- coarse_out: bfloat16 [128, 128, 256], P('gx', 'gy')
- grad_conv: float32 [7, 64, 64], replicated
- grad_time: float32 [64, 64], replicated
- grad_up: float32 [64, 256], replicated
- grad_kernel: float32 [9, 256, 256], replicated
- grad_out: float32 [256, 256], replicated
Inputs may be any that keep to these rules, and one draw needn't show every extreme that they name: An entry is a brick number or -1 for no neighbour. The lists are symmetric: neighbours[n, f] = j >= 0 exactly when neighbours[j, g] = n, with g the face opposite to f (f xor 1). Brick n lies on device n // 64 of gx+gy. An entry of face 2 k of a brick on device i (k = 0, 1, 2) names a brick of device i or of device (i + d) modulo the device count, and an entry of face 2 k + 1 one of device i or (i - d) modulo the device count, with d in k * 2 + 1 .. (k + 1) * 2. For each face and each such d, exactly 12 entries of one device's bricks name bricks of that other device. `parent_dev`: among the 64 bricks of one device at most 2 have the same value, and some device reaches that.
All inputs are finite; a program needn't handle non-finite values.
Results may differ from a plain program's by a relative error of at most 0.0075.
Values may be sent and summed in bfloat16 or wider, within the bound.
A program may use at most 256 MiB of HBM per device.

v0:
```python
import math

import jax
import jax.numpy as jnp
from jax import lax
from jax.sharding import PartitionSpec as P

KOFF = 2
MFACE = 12


def passed_along(value, axis, steps):
    count = lax.axis_size(axis)
    pairs = [(source, (source + steps) % count) for source in range(count)]
    return lax.ppermute(value, axis, pairs)


def extended(cells, sides, width):
    for axis, dim in sides:
        count = lax.axis_size(axis)
        ends = count - 1
        head = lax.slice_in_dim(cells, 0, width, axis=dim)
        tail = lax.slice_in_dim(cells, cells.shape[dim] - width, cells.shape[dim], axis=dim)
        cells = jnp.concatenate(
            [
                lax.ppermute(tail, axis, [(i, (i + 1) % count) for i in range(ends)]),
                cells,
                lax.ppermute(head, axis, [((i + 1) % count, i) for i in range(ends)]),
            ],
            axis=dim,
        )
    return cells


def time_features(timestep, channels):
    half_count = channels // 2
    frequency = jnp.exp(-math.log(10000.0) * jnp.arange(half_count, dtype=jnp.float32) / half_count)
    angles = timestep[0].astype(jnp.float32) * frequency
    return jnp.concatenate([jnp.sin(angles), jnp.cos(angles)])


def silu_grad(values):
    sigma = jax.nn.sigmoid(values)
    return sigma * (1.0 + values * (1.0 - sigma))


def face_planes(field):
    bricks, channels, voxels = field.shape
    volume = field.reshape(bricks, channels, 8, 8, 8)
    faces_list = [
        volume[:, :, 7],
        volume[:, :, 0],
        volume[:, :, :, 7],
        volume[:, :, :, 0],
        volume[:, :, :, :, 7],
        volume[:, :, :, :, 0],
    ]
    return jnp.stack(faces_list, axis=1).reshape(bricks, 6, channels * 64)


def spread_plane(face_plane, missing):
    bricks, channels = (face_plane.shape[0], face_plane.shape[1])
    if missing == 1:
        shaped = face_plane.reshape(bricks, channels, 8, 1, 8)
    else:
        shaped = face_plane.reshape(bricks, channels, 8, 8, 1)
    return jnp.broadcast_to(shaped, (bricks, channels, 8, 8, 8)).reshape(bricks, channels, 512)


def shifted_list(field, nearby):
    voxels = field.shape[2]
    position = jnp.arange(voxels)
    index_y = position // 8 % 8
    index_z = position % 8
    zeros_eight = jnp.zeros_like(field[..., :8])
    zeros_one = jnp.zeros_like(field[..., :1])
    plus_x = jnp.concatenate([field[..., 64:], nearby[:, 0]], axis=-1)
    minus_x = jnp.concatenate([nearby[:, 1], field[..., : voxels - 64]], axis=-1)
    plus_y = jnp.where(
        index_y == 7,
        spread_plane(nearby[:, 2], 1),
        jnp.concatenate([field[..., 8:], zeros_eight], axis=-1),
    )
    minus_y = jnp.where(
        index_y == 0,
        spread_plane(nearby[:, 3], 1),
        jnp.concatenate([zeros_eight, field[..., : voxels - 8]], axis=-1),
    )
    plus_z = jnp.where(
        index_z == 7,
        spread_plane(nearby[:, 4], 2),
        jnp.concatenate([field[..., 1:], zeros_one], axis=-1),
    )
    minus_z = jnp.where(
        index_z == 0,
        spread_plane(nearby[:, 5], 2),
        jnp.concatenate([zeros_one, field[..., : voxels - 1]], axis=-1),
    )
    return [field, plus_x, minus_x, plus_y, minus_y, plus_z, minus_z]


def slot_ranks(hot):
    return jnp.sum(jnp.cumsum(hot, axis=0) * hot, axis=1) - 1


def fill_slots(values, slot_id, slot_total, empty_value):
    row_count = values.shape[0]
    source = (
        jnp.full((slot_total,), row_count, jnp.int32)
        .at[slot_id]
        .set(jnp.arange(row_count, dtype=jnp.int32), mode="drop")
    )
    fetched = values[jnp.minimum(source, row_count - 1)]
    used = (source < row_count).reshape((slot_total,) + (1,) * (values.ndim - 1))
    return jnp.where(used, fetched, jnp.full_like(fetched, empty_value))


def shards(
    fine_in,
    neighbours,
    parent_dev,
    parent_cell,
    timestep,
    conv_weight,
    time_weight,
    up_weight,
    coarse_in,
    coarse_kernel,
    out_weight,
    coarse_cot,
):
    bricks, channels, voxels = fine_in.shape
    plane_width = channels * 64
    count_x = lax.axis_size("gx")
    count_y = lax.axis_size("gy")
    device_count = count_x * count_y
    myself = lax.axis_index("gx") * count_y + lax.axis_index("gy")
    peer_ids = jnp.arange(device_count, dtype=jnp.int32)
    time_basis = time_features(timestep, channels)
    embedding = jnp.dot(time_weight, time_basis, precision=lax.Precision.HIGHEST)
    planes = face_planes(fine_in).reshape(bricks * 6, plane_width)
    flat_nb = neighbours.reshape(-1)
    present = flat_nb >= 0
    holder = jnp.where(present, flat_nb // bricks, myself)
    remote = present & (holder != myself)
    target = jnp.where(remote, holder, device_count)
    facing = jnp.arange(bricks * 6, dtype=jnp.int32) % 6
    opposite = facing + 1 - 2 * (facing % 2)
    wanted = jnp.where(present, flat_nb % bricks, 0) * 6 + opposite
    same_source = target[None, :] == target[:, None]
    earlier = wanted[None, :] < wanted[:, None]
    order_in = jnp.sum((same_source & earlier).astype(jnp.int32), axis=1)
    gap_values = [step for step in range(1, 3 * KOFF + 1)] + [
        -step for step in range(1, 3 * KOFF + 1)
    ]
    gap_count = len(gap_values)
    gap_table = jnp.array([value % device_count for value in gap_values], jnp.int32)
    gap_ids = jnp.arange(gap_count, dtype=jnp.int32)
    send_hot = (((target - myself) % device_count)[:, None] == gap_table[None, :]) & remote[:, None]
    send_hot = send_hot.astype(jnp.int32)
    send_bucket = jnp.sum(send_hot * gap_ids[None, :], axis=1)
    send_slot = slot_ranks(send_hot)
    send_id = jnp.where(
        remote & (send_slot < MFACE), send_bucket * MFACE + send_slot, gap_count * MFACE
    )
    buckets_out = fill_slots(planes, send_id, gap_count * MFACE, 0).reshape(
        gap_count, MFACE, plane_width
    )
    received = [
        passed_along(buckets_out[bucket_id], ("gx", "gy"), gap_values[bucket_id])
        for bucket_id in range(gap_count)
    ]
    arrived = jnp.stack(received, axis=0).reshape(gap_count * MFACE, plane_width)
    recv_hot = (((myself - holder) % device_count)[:, None] == gap_table[None, :]).astype(jnp.int32)
    recv_bucket = jnp.sum(recv_hot * gap_ids[None, :], axis=1)
    from_far = arrived[
        jnp.minimum(recv_bucket, gap_count - 1) * MFACE + jnp.minimum(order_in, MFACE - 1)
    ]
    from_near = planes[wanted]
    nearby = jnp.where(
        remote[:, None], from_far, jnp.where(present[:, None], from_near, jnp.zeros_like(from_near))
    )
    nearby = nearby.reshape(bricks, 6, channels, 64)
    shifted = shifted_list(fine_in, nearby)
    hidden = jnp.einsum(
        "oc,bcv->bov", conv_weight[0], shifted[0], preferred_element_type=jnp.float32
    )
    for tap_index in range(1, 7):
        hidden = hidden + jnp.einsum(
            "oc,bcv->bov",
            conv_weight[tap_index],
            shifted[tap_index],
            preferred_element_type=jnp.float32,
        )
    hidden = hidden + embedding[None, :, None]
    activated = jax.nn.silu(hidden)
    fine_act = activated.astype(jnp.bfloat16)
    pooled = jnp.mean(activated, axis=-1).astype(jnp.bfloat16)
    lifted = jnp.dot(pooled, up_weight, preferred_element_type=jnp.float32).astype(jnp.bfloat16)
    capacity = max(2, 2 * bricks // device_count)
    owners = parent_dev[:, 0]
    owner_hot = (owners[:, None] == peer_ids[None, :]).astype(jnp.int32)
    row_place = slot_ranks(owner_hot)
    row_id = owners * capacity + row_place
    rows_out = fill_slots(lifted, row_id, device_count * capacity, 0).reshape(
        device_count, capacity, lifted.shape[1]
    )
    cells_out = fill_slots(parent_cell, row_id, device_count * capacity, -1).reshape(
        device_count, capacity
    )
    rows_in, cells_in = (
        lax.all_to_all(rows_out, ("gx", "gy"), split_axis=0, concat_axis=0, tiled=True),
        lax.all_to_all(cells_out, ("gx", "gy"), split_axis=0, concat_axis=0, tiled=True),
    )
    rows_in = rows_in.reshape(device_count * capacity, -1)
    tile_x, tile_y, coarse_width = coarse_in.shape
    cell_hot = (
        cells_in.reshape(-1)[:, None] == jnp.arange(tile_x * tile_y, dtype=jnp.int32)[None, :]
    ).astype(jnp.bfloat16)
    injected = jnp.einsum("rc,rw->cw", cell_hot, rows_in, preferred_element_type=jnp.float32)
    coarse_value = coarse_in.astype(jnp.float32).reshape(-1, coarse_width)
    rim_values = (
        jax.nn.silu(coarse_value).astype(jnp.bfloat16).reshape(tile_x, tile_y, coarse_width)
    )
    padded = extended(rim_values, (("gx", 0), ("gy", 1)), 1)
    tap_rows = [
        padded[offset_row : offset_row + tile_x, offset_col : offset_col + tile_y].reshape(
            -1, coarse_width
        )
        for offset_row in range(3)
        for offset_col in range(3)
    ]
    convolved = jnp.zeros((tile_x * tile_y, coarse_width), jnp.float32)
    for tap_index in range(9):
        convolved = convolved + jnp.dot(
            tap_rows[tap_index], coarse_kernel[tap_index], preferred_element_type=jnp.float32
        )
    coarse_pre = coarse_value + convolved + injected
    coarse_act = jax.nn.silu(coarse_pre).astype(jnp.bfloat16)
    coarse_out = (
        (coarse_pre + jnp.dot(coarse_act, out_weight, preferred_element_type=jnp.float32))
        .astype(jnp.bfloat16)
        .reshape(tile_x, tile_y, coarse_width)
    )
    loss_scale = 1.0 / math.sqrt(tile_x * count_x * tile_y * count_y)
    grad_outs = (coarse_cot.astype(jnp.float32).reshape(-1, coarse_width) * loss_scale).astype(
        jnp.bfloat16
    )
    through = jnp.dot(grad_outs, out_weight.T, preferred_element_type=jnp.float32)
    grad_pre = (grad_outs.astype(jnp.float32) + through * silu_grad(coarse_pre)).astype(
        jnp.bfloat16
    )
    grad_out = jnp.einsum("rc,rw->cw", coarse_act, grad_outs, preferred_element_type=jnp.float32)
    grad_kernel = jnp.stack(
        [
            jnp.einsum(
                "rc,rw->cw", tap_rows[tap_index], grad_pre, preferred_element_type=jnp.float32
            )
            for tap_index in range(9)
        ]
    )
    grad_slots = jnp.dot(cell_hot, grad_pre, preferred_element_type=jnp.float32).astype(
        jnp.bfloat16
    )
    back_rows = lax.all_to_all(
        grad_slots.reshape(device_count, capacity, -1),
        ("gx", "gy"),
        split_axis=0,
        concat_axis=0,
        tiled=True,
    )
    back_rows = back_rows.reshape(device_count * capacity, -1)
    my_rows = back_rows[row_id]
    grad_up_part = jnp.einsum("bc,bw->cw", pooled, my_rows, preferred_element_type=jnp.float32)
    grad_pooled = jnp.dot(my_rows, up_weight.T, preferred_element_type=jnp.float32).astype(
        jnp.bfloat16
    )
    grad_hidden = grad_pooled.astype(jnp.float32)[:, :, None] / voxels * silu_grad(hidden)
    grad_hidden_low = grad_hidden.astype(jnp.bfloat16)
    grad_conv = jnp.stack(
        [
            jnp.einsum(
                "bov,bcv->oc",
                grad_hidden_low,
                shifted[tap_index],
                preferred_element_type=jnp.float32,
            )
            for tap_index in range(7)
        ]
    )
    grad_time = jnp.outer(jnp.sum(grad_hidden, axis=(0, 2)), time_basis)
    totals = lax.psum((grad_conv, grad_time, grad_up_part, grad_kernel, grad_out), ("gx", "gy"))
    return (fine_act, coarse_out, totals[0], totals[1], totals[2], totals[3], totals[4])


def solution(mesh):
    return jax.shard_map(
        shards,
        mesh=mesh,
        in_specs=(
            P(("gx", "gy"), None, None),
            P(("gx", "gy"), None),
            P(("gx", "gy"), None),
            P(("gx", "gy")),
            P(),
            P(),
            P(),
            P(),
            P("gx", "gy", None),
            P(),
            P(),
            P("gx", "gy", None),
        ),
        out_specs=(P(("gx", "gy"), None, None), P("gx", "gy", None), P(), P(), P(), P(), P()),
        check_vma=False,
    )
```

profile of v0, /device:TPU:1, one launch (start us, length us, event | category | flops | bytes accessed | tf_op | source)
XLA Modules:
  0.0 634.3 jit_solution(14699762455136379667)
XLA Ops:
  7.2 8.4 %copy.147 = bf16[64,64,512]{1,2,0:T(8,128)(2,1)} copy(bf16[64,64,512]{2,1,0:T(8,128)(2,1)} %param.13) | data formatting | bytes 8388608 | tf_op args[0]
  17.9 10.5 %fusion.171 = (bf16[64,64,8,8,1]{1,4,3,2,0:T(2,128)(2,1)S(1)}, bf16[64,64,8,8,1]{1,4,3,2,0:T(2,128)(2,1)}) fusion(bf16[64,64,8,8,8]{1,4,3,2,0:T(8,128)(2,1)} %bitcast.354), kind=kLoop, calls=%fused_computation.344 | loop fusion | bytes 2097152 | tf_op jit(solution)/shard_map/slice | solution.py:56
  43.1 37.2 %copy.153 = bf16[64,6,64,8,8]{4,3,2,1,0:T(8,128)(2,1)} copy(bf16[64,6,64,8,8]{2,4,3,0,1:T(8,128)(2,1)} %bitcast_dynamic-update-slice_fusion) | data formatting | bytes 6291456 | tf_op jit(solution)/shard_map/stack | solution.py:58
  80.3 70.9 %reshape_reshape.3 = bf16[384,4096]{1,0:T(8,128)(2,1)S(1)} reshape(bf16[64,6,64,8,8]{4,3,2,1,0:T(8,128)(2,1)} %copy.153) | data formatting | bytes 6291456 | tf_op jit(solution)/shard_map/reshape;reshape | solution.py:141
  174.7 6.8 %all-to-all-start = ((s32[128,1,2]{2,1,0:T(1,128)}), s32[128,1,2]{2,1,0:T(1,128)S(1)}, u32[]{:S(2)}, u32[]{:S(2)}) async-start(s32[128,1,2]{2,1,0:T(1,128)} %bitcast.72), calls=%async_computation | async-start | bytes 131072 | tf_op jit(solution)/shard_map/all_to_all | solution.py:213
  181.5 13.4 %fusion.169 = (bf16[64,64,511]{1,2,0:T(8,128)(2,1)}, bf16[64,64,511]{1,2,0:T(8,128)(2,1)}) fusion(bf16[64,64,512]{1,2,0:T(8,128)(2,1)} %copy.147), kind=kLoop, calls=%fused_computation.342 | loop fusion | bytes 16744448 | tf_op jit(solution)/shard_map/slice | solution.py:97
  196.6 11.8 %fusion.170 = (bf16[64,64,504]{1,2,0:T(8,128)(2,1)}, bf16[64,64,504]{1,2,0:T(8,128)(2,1)}) fusion(bf16[64,64,512]{1,2,0:T(8,128)(2,1)} %copy.147), kind=kLoop, calls=%fused_computation.343 | loop fusion | bytes 16515072 | tf_op jit(solution)/shard_map/slice | solution.py:82
  209.0 4.6 fusion.173
  215.6 5.2 fusion.96
  226.2 9.8 %gather.28 = bf16[64,6,64,64]{3,2,1,0:T(8,128)(2,1)} reshape(bf16[384,4096]{1,0:T(8,128)(2,1)} %gather_fusion.2) | data formatting | bytes 6291456 | tf_op jit(solution)/shard_map/gather | solution.py:179
  252.6 4.7 collective-permute-start.5
  265.9 4.2 collective-permute-start.10
  270.1 5.0 collective-permute-start.11
  279.9 4.2 gather_fusion.1
  284.0 9.7 %gather.26 = bf16[64,6,64,64]{3,2,1,0:T(8,128)(2,1)} reshape(bf16[384,4096]{1,0:T(8,128)(2,1)} %gather_fusion.1) | data formatting | bytes 6291456 | tf_op jit(solution)/shard_map/gather | solution.py:176
  293.7 5.4 copy_select_fusion
  306.0 6.5 %bitcast_select_fusion.1 = bf16[64,64,512]{1,2,0:T(8,128)(2,1)S(1)} fusion(bf16[64,64,511]{1,2,0:T(8,128)(2,1)} %get-tuple-element.29, pred[512]{0:T(512)(128)(4,1)} %broadcast_compare_fusion.3, bf16[64,64,8,8]{1,3,2,0:T(8,128)(2,1)} %bitcast.370), kind=kLoop, calls=%fused_computation.18 | loop fusion | flops 2097152 | bytes 8905216 | tf_op jit(solution)/shard_map/jit(_where)/select_n | solution.py:89
  312.5 7.0 %fusion.88 = f32[64,512,64]{1,2,0:T(8,128)} fusion(bf16[64,64,512]{1,2,0:T(8,128)(2,1)S(1)} %bitcast_select_fusion.1, bf16[7,64,64]{2,1,0:T(8,128)(2,1)} %param.18), kind=kOutput, calls=%fused_computation.182 | convolution fusion | flops 268435456 | bytes 12599296 | tf_op jit(solution)/shard_map/oc,bcv->bov/dot_general | solution.py:189
  320.9 10.4 %bitcast_select_fusion.2 = bf16[64,64,512]{1,2,0:T(8,128)(2,1)} fusion(bf16[64,64,504]{1,2,0:T(8,128)(2,1)} %get-tuple-element.31, pred[512]{0:T(512)(128)(4,1)} %broadcast_compare_fusion.2, bf16[64,64,8,8]{1,3,2,0:T(8,128)(2,1)} %bitcast.371), kind=kLoop, calls=%fused_computation.19 | loop fusion | flops 2097152 | bytes 8847872 | tf_op jit(solution)/shard_map/jit(_where)/select_n | solution.py:84
  331.2 9.7 %fusion.90 = f32[64,512,64]{1,2,0:T(8,128)} fusion(bf16[64,64,512]{1,2,0:T(8,128)(2,1)} %bitcast_select_fusion.2, bf16[7,64,64]{2,1,0:T(8,128)(2,1)} %param.18), kind=kOutput, calls=%fused_computation.184 | convolution fusion | flops 268435456 | bytes 16793600 | tf_op jit(solution)/shard_map/oc,bcv->bov/dot_general | solution.py:189
  341.7 9.4 %bitcast_select_fusion.3 = bf16[64,64,512]{1,2,0:T(8,128)(2,1)} fusion(bf16[64,64,504]{1,2,0:T(8,128)(2,1)} %get-tuple-element.30, pred[512]{0:T(512)(128)(4,1)} %broadcast_compare_fusion.4, bf16[64,64,8,8]{1,3,2,0:T(8,128)(2,1)S(1)} %bitcast.369), kind=kLoop, calls=%fused_computation.20 | loop fusion | flops 2097152 | bytes 8847872 | tf_op jit(solution)/shard_map/jit(_where)/select_n | solution.py:79
  351.1 9.8 %fusion.92 = f32[64,512,64]{1,2,0:T(8,128)} fusion(bf16[64,64,512]{1,2,0:T(8,128)(2,1)} %bitcast_select_fusion.3, bf16[7,64,64]{2,1,0:T(8,128)(2,1)} %param.18), kind=kOutput, calls=%fused_computation.186 | convolution fusion | flops 268435456 | bytes 16793600 | tf_op jit(solution)/shard_map/oc,bcv->bov/dot_general | solution.py:189
  360.9 5.7 fusion.7
  366.7 5.5 fusion.9
  372.2 6.8 %bitcast_select_fusion = bf16[64,64,512]{1,2,0:T(8,128)(2,1)} fusion(bf16[64,64,511]{1,2,0:T(8,128)(2,1)S(1)} %bitcast.367, pred[512]{0:T(512)(128)(4,1)S(1)} %copy-done.40, bf16[64,64,8,8]{1,3,2,0:T(8,128)(2,1)S(1)} %bitcast.368), kind=kLoop, calls=%fused_computation.17 | loop fusion | flops 2097152 | bytes 8905216 | tf_op jit(solution)/shard_map/jit(_where)/select_n | solution.py:94
  379.1 23.4 %fusion.10 = (f32[64,64]{1,0:T(8,128)S(1)}, f32[64,512,64]{1,2,0:T(8,128)}) fusion(f32[64]{0:T(128)S(1)} %copy-done.39, bf16[64,64,512]{1,2,0:T(8,128)(2,1)} %bitcast_select_fusion, bf16[7,64,64]{2,1,0:T(8,128)(2,1)} %param.18, f32[64,512,64]{1,2,0:T(8,128)} %fusion.88, f32[64,512,64]{1,2,0:T(8,128)} %fusion.90, f32[64,512,64]{1,2,0:T(8,128)} %fusion.92, ...), kind=kOutput, calls=%fused_computation.30 | convolution fusion | flops 293597184 | bytes 67141888 | tf_op jit(solution)/shard_map/oc,bcv->bov/dot_general | solution.py:189
  404.8 9.2 %all-to-all-start.1 = ((bf16[128,2,256]{2,1,0:T(2,128)(2,1)}), bf16[128,2,256]{2,1,0:T(2,128)(2,1)S(1)}, u32[]{:S(2)}, u32[]{:S(2)}) async-start(bf16[128,2,256]{2,1,0:T(2,128)(2,1)} %broadcast_select_fusion.1), calls=%async_computation.1 | async-start | bytes 262144 | tf_op jit(solution)/shard_map/all_to_all | solution.py:212
  415.2 8.9 %all-to-all-done.1 = bf16[128,2,256]{2,1,0:T(2,128)(2,1)S(1)} async-done(((bf16[128,2,256]{2,1,0:T(2,128)(2,1)}), bf16[128,2,256]{2,1,0:T(2,128)(2,1)S(1)}, u32[]{:S(2)}, u32[]{:S(2)}) %all-to-all-start.1) | async-done | bytes 131104 | tf_op jit(solution)/shard_map/all_to_all | solution.py:212
  427.5 4.2 all-to-all-start.2
  443.6 7.9 %fusion.166 = (f32[64]{0:T(128)S(1)}, bf16[64,64,512]{2,1,0:T(8,128)(2,1)S(1)}, bf16[64,64,512]{2,1,0:T(8,128)(2,1)}) fusion(f32[64,512,64]{1,2,0:T(8,128)} %get-tuple-element.64, f32[64,64]{1,0:T(8,128)S(1)} %fusion.37), kind=kLoop, calls=%fused_computation.340 | loop fusion | flops 25165760 | bytes 16793856 | tf_op jit(solution)/shard_map/reduce_sum | solution.py:291
  468.6 64.7 %psum.36 = f32[64,64]{1,0:T(8,128)} all-reduce(f32[64,64]{1,0:T(8,128)S(1)} %broadcast_multiply_fusion), channel_id=1, replica_groups=mesh['gx'=8,'gy'=16] {'gx','gy'}, use_global_device_ids=true, to_apply=%region_13.14 | all-reduce | flops 4096 | bytes 32768 | tf_op jit(solution)/shard_map/psum | solution.py:292
  533.3 86.6 %all-reduce.7.cloned.1.call-done = (f32[7,64,64]{2,1,0:T(8,128)}, f32[64,256]{1,0:T(8,128)}, f32[9,256,256]{2,1,0:T(8,128)}, f32[256,256]{1,0:T(8,128)}) async-done(((f32[7,64,64]{2,1,0:T(8,128)}, f32[64,256]{1,0:T(8,128)}, f32[9,256,256]{2,1,0:T(8,128)}, f32[256,256]{1,0:T(8,128)}), (f32[7,64,64]{2,1,0:T(8,128)}, f32[64,256]{1,0:T(8,128)}, f32[9,256,256]{2,1,0:T(8,128)}, ...) | async-done | bytes 2801680 | tf_op jit(solution)/shard_map/psum | solution.py:292
  (272 shorter events, 130.6 us)
Async XLA Ops:
  7.2 417.3 %copy-start = (bf16[256,256]{1,0:T(8,128)(2,1)S(1)}, bf16[256,256]{1,0:T(8,128)(2,1)}, u32[]{:S(2)}) copy-start(bf16[256,256]{1,0:T(8,128)(2,1)} %param.23) | copy-start | bytes 393220
  156.2 96.4 %collective-permute-start = (bf16[12,4096]{1,0:T(8,128)(2,1)}, bf16[12,4096]{1,0:T(8,128)(2,1)}, u32[]{:S(2)}, u32[]{:S(2)}) collective-permute-start(bf16[12,4096]{1,0:T(8,128)(2,1)} %get-tuple-element.53), channel_id=1, source_target_pairs={{0,1},{1,2},{2,3},{3,4},{4,5},{5,6},{6,7},{7,8},{8,9},{9,10},{10,1... | collective-permute-start | bytes 294920 | tf_op jit(solution)/shard_map/ppermute | solution.py:15
  158.7 99.6 %collective-permute-start.1 = (bf16[12,4096]{1,0:T(8,128)(2,1)}, bf16[12,4096]{1,0:T(8,128)(2,1)}, u32[]{:S(2)}, u32[]{:S(2)}) collective-permute-start(bf16[12,4096]{1,0:T(8,128)(2,1)} %get-tuple-element.52), channel_id=1, source_target_pairs={{0,2},{1,3},{2,4},{3,5},{4,6},{5,7},{6,8},{7,9},{8,10},{9,11},{10,... | collective-permute-start | bytes 294920 | tf_op jit(solution)/shard_map/ppermute | solution.py:15
  162.0 99.5 %collective-permute-start.2 = (bf16[12,4096]{1,0:T(8,128)(2,1)}, bf16[12,4096]{1,0:T(8,128)(2,1)}, u32[]{:S(2)}, u32[]{:S(2)}) collective-permute-start(bf16[12,4096]{1,0:T(8,128)(2,1)} %get-tuple-element.51), channel_id=1, source_target_pairs={{0,3},{1,4},{2,5},{3,6},{4,7},{5,8},{6,9},{7,10},{8,11},{9,12},{10... | collective-permute-start | bytes 294920 | tf_op jit(solution)/shard_map/ppermute | solution.py:15
  164.3 74.5 %collective-permute-start.13 = (bf16[1,8,256]{2,1,0:T(8,128)(2,1)}, bf16[1,8,256]{2,1,0:T(8,128)(2,1)S(1)}, u32[]{:S(2)}, u32[]{:S(2)}) collective-permute-start(bf16[1,8,256]{2,1,0:T(8,128)(2,1)} %get-tuple-element.59), channel_id=1, source_target_pairs={{16,0},{32,16},{48,32},{64,48},{80,64},{96,80},{112,96},{17,1},{33... | collective-permute-start | bytes 12296 | tf_op jit(solution)/shard_map/ppermute | solution.py:28
  167.8 71.1 %collective-permute-start.12 = (bf16[1,8,256]{2,1,0:T(8,128)(2,1)}, bf16[1,8,256]{2,1,0:T(8,128)(2,1)S(1)}, u32[]{:S(2)}, u32[]{:S(2)}) collective-permute-start(bf16[1,8,256]{2,1,0:T(8,128)(2,1)} %get-tuple-element.58), channel_id=1, source_target_pairs={{0,16},{16,32},{32,48},{48,64},{64,80},{80,96},{96,112},{1,17},{17... | collective-permute-start | bytes 12296 | tf_op jit(solution)/shard_map/ppermute | solution.py:26
  174.7 62.1 %all-to-all-start = ((s32[128,1,2]{2,1,0:T(1,128)}), s32[128,1,2]{2,1,0:T(1,128)S(1)}, u32[]{:S(2)}, u32[]{:S(2)}) async-start(s32[128,1,2]{2,1,0:T(1,128)} %bitcast.72), calls=%async_computation | async-start | bytes 131072 | tf_op jit(solution)/shard_map/all_to_all | solution.py:213
  236.0 28.3 %copy-start.22 = (bf16[12,4096]{1,0:T(8,128)(2,1)S(1)}, bf16[12,4096]{1,0:T(8,128)(2,1)}, u32[]{:S(2)}) copy-start(bf16[12,4096]{1,0:T(8,128)(2,1)} %get-tuple-element.44) | copy-start | bytes 294916
  236.0 29.9 %copy-start.21 = (bf16[12,4096]{1,0:T(8,128)(2,1)S(1)}, bf16[12,4096]{1,0:T(8,128)(2,1)}, u32[]{:S(2)}) copy-start(bf16[12,4096]{1,0:T(8,128)(2,1)} %get-tuple-element.43) | copy-start | bytes 294916
  236.0 34.1 %copy-start.20 = (bf16[12,4096]{1,0:T(8,128)(2,1)S(1)}, bf16[12,4096]{1,0:T(8,128)(2,1)}, u32[]{:S(2)}) copy-start(bf16[12,4096]{1,0:T(8,128)(2,1)} %get-tuple-element.42) | copy-start | bytes 294916
  238.9 4.9 collective-permute-start.14
  242.3 5.6 collective-permute-start.15
  243.8 20.4 %collective-permute-start.3 = (bf16[12,4096]{1,0:T(8,128)(2,1)}, bf16[12,4096]{1,0:T(8,128)(2,1)S(1)}, u32[]{:S(2)}, u32[]{:S(2)}) collective-permute-start(bf16[12,4096]{1,0:T(8,128)(2,1)} %get-tuple-element.50), channel_id=1, source_target_pairs={{0,4},{1,5},{2,6},{3,7},{4,8},{5,9},{6,10},{7,11},{8,12},{9,13},{1... | collective-permute-start | bytes 294920 | tf_op jit(solution)/shard_map/ppermute | solution.py:15
  248.0 16.3 %collective-permute-start.4 = (bf16[12,4096]{1,0:T(8,128)(2,1)}, bf16[12,4096]{1,0:T(8,128)(2,1)S(1)}, u32[]{:S(2)}, u32[]{:S(2)}) collective-permute-start(bf16[12,4096]{1,0:T(8,128)(2,1)} %get-tuple-element.49), channel_id=1, source_target_pairs={{0,5},{1,6},{2,7},{3,8},{4,9},{5,10},{6,11},{7,12},{8,13},{9,14},{... | collective-permute-start | bytes 294920 | tf_op jit(solution)/shard_map/ppermute | solution.py:15
  250.1 29.4 %copy-start.12 = (bf16[18,9,256]{2,1,0:T(8,128)(2,1)}, bf16[18,9,256]{2,1,0:T(8,128)(2,1)S(1)}, u32[]{:S(2)}) copy-start(bf16[18,9,256]{2,1,0:T(8,128)(2,1)S(1)} %get-tuple-element.54) | copy-start | bytes 248836
  252.6 13.3 %collective-permute-start.5 = (bf16[12,4096]{1,0:T(8,128)(2,1)}, bf16[12,4096]{1,0:T(8,128)(2,1)S(1)}, u32[]{:S(2)}, u32[]{:S(2)}) collective-permute-start(bf16[12,4096]{1,0:T(8,128)(2,1)} %get-tuple-element.48), channel_id=1, source_target_pairs={{0,6},{1,7},{2,8},{3,9},{4,10},{5,11},{6,12},{7,13},{8,14},{9,15},... | collective-permute-start | bytes 294920 | tf_op jit(solution)/shard_map/ppermute | solution.py:15
  258.3 11.9 %collective-permute-start.6 = (bf16[12,4096]{1,0:T(8,128)(2,1)}, bf16[12,4096]{1,0:T(8,128)(2,1)S(1)}, u32[]{:S(2)}, u32[]{:S(2)}) collective-permute-start(bf16[12,4096]{1,0:T(8,128)(2,1)} %get-tuple-element.47), channel_id=1, source_target_pairs={{0,127},{1,0},{2,1},{3,2},{4,3},{5,4},{6,5},{7,6},{8,7},{9,8},{10,... | collective-permute-start | bytes 294920 | tf_op jit(solution)/shard_map/ppermute | solution.py:15
  261.4 13.7 %collective-permute-start.7 = (bf16[12,4096]{1,0:T(8,128)(2,1)}, bf16[12,4096]{1,0:T(8,128)(2,1)S(1)}, u32[]{:S(2)}, u32[]{:S(2)}) collective-permute-start(bf16[12,4096]{1,0:T(8,128)(2,1)} %get-tuple-element.46), channel_id=1, source_target_pairs={{0,126},{1,127},{2,0},{3,1},{4,2},{5,3},{6,4},{7,5},{8,6},{9,7},{1... | collective-permute-start | bytes 294920 | tf_op jit(solution)/shard_map/ppermute | solution.py:15
  264.2 12.4 %collective-permute-start.8 = (bf16[12,4096]{1,0:T(8,128)(2,1)}, bf16[12,4096]{1,0:T(8,128)(2,1)S(1)}, u32[]{:S(2)}, u32[]{:S(2)}) collective-permute-start(bf16[12,4096]{1,0:T(8,128)(2,1)} %get-tuple-element.45), channel_id=1, source_target_pairs={{0,125},{1,126},{2,127},{3,0},{4,1},{5,2},{6,3},{7,4},{8,5},{9,6},... | collective-permute-start | bytes 294920 | tf_op jit(solution)/shard_map/ppermute | solution.py:15
  264.3 15.1 %collective-permute-start.9 = (bf16[12,4096]{1,0:T(8,128)(2,1)S(1)}, bf16[12,4096]{1,0:T(8,128)(2,1)S(1)}, u32[]{:S(2)}, u32[]{:S(2)}) collective-permute-start(bf16[12,4096]{1,0:T(8,128)(2,1)S(1)} %copy-done.22), channel_id=1, source_target_pairs={{0,124},{1,125},{2,126},{3,127},{4,0},{5,1},{6,2},{7,3},{8,4},{9,5... | collective-permute-start | bytes 294920 | tf_op jit(solution)/shard_map/ppermute | solution.py:15
  265.9 13.6 %collective-permute-start.10 = (bf16[12,4096]{1,0:T(8,128)(2,1)S(1)}, bf16[12,4096]{1,0:T(8,128)(2,1)S(1)}, u32[]{:S(2)}, u32[]{:S(2)}) collective-permute-start(bf16[12,4096]{1,0:T(8,128)(2,1)S(1)} %copy-done.21), channel_id=1, source_target_pairs={{0,123},{1,124},{2,125},{3,126},{4,127},{5,0},{6,1},{7,2},{8,3},{9... | collective-permute-start | bytes 294920 | tf_op jit(solution)/shard_map/ppermute | solution.py:15
  270.1 9.4 %collective-permute-start.11 = (bf16[12,4096]{1,0:T(8,128)(2,1)S(1)}, bf16[12,4096]{1,0:T(8,128)(2,1)S(1)}, u32[]{:S(2)}, u32[]{:S(2)}) collective-permute-start(bf16[12,4096]{1,0:T(8,128)(2,1)S(1)} %copy-done.20), channel_id=1, source_target_pairs={{0,122},{1,123},{2,124},{3,125},{4,126},{5,127},{6,0},{7,1},{8,2},... | collective-permute-start | bytes 294920 | tf_op jit(solution)/shard_map/ppermute | solution.py:15
  379.0 24.9 %copy-start.28 = (pred[128,2]{1,0:T(8,128)(4,1)S(1)}, pred[128,2]{1,0:T(8,128)(4,1)}, u32[]{:S(2)}) copy-start(pred[128,2]{1,0:T(8,128)(4,1)} %broadcast_in_dim.165) | copy-start | bytes 772
  379.0 35.1 %copy-start.16 = (f32[128,256]{1,0:T(8,128)S(1)}, f32[128,256]{1,0:T(8,128)}, u32[]{:S(2)}) copy-start(f32[128,256]{1,0:T(8,128)} %convolution_add_fusion.3) | copy-start | bytes 393220
  379.0 35.1 %copy-start.17 = (f32[128,256]{1,0:T(8,128)S(1)}, f32[128,256]{1,0:T(8,128)}, u32[]{:S(2)}) copy-start(f32[128,256]{1,0:T(8,128)} %fusion.52) | copy-start | bytes 393220
  379.0 35.1 %copy-start.25 = (bf16[1,8,256]{2,1,0:T(8,128)(2,1)S(1)}, bf16[1,8,256]{2,1,0:T(8,128)(2,1)}, u32[]{:S(2)}) copy-start(bf16[1,8,256]{2,1,0:T(8,128)(2,1)} %copy-done.24) | copy-start | bytes 12292
  379.0 45.1 %copy-start.31 = (s32[256]{0:T(256)S(1)}, s32[256]{0:T(256)}, u32[]{:S(2)}) copy-start(s32[256]{0:T(256)} %eq.115) | copy-start | bytes 3076
  379.1 45.4 %copy-start.41 = (bf16[16,8,256]{2,1,0:T(8,128)(2,1)S(1)}, bf16[16,8,256]{2,1,0:T(8,128)(2,1)}, u32[]{:S(2)}) copy-start(bf16[16,8,256]{2,1,0:T(8,128)(2,1)} %param.24) | copy-start | bytes 196612
  402.4 29.3 %copy-start.27 = (bf16[1,8,256]{2,1,0:T(8,128)(2,1)S(1)}, bf16[1,8,256]{2,1,0:T(8,128)(2,1)}, u32[]{:S(2)}) copy-start(bf16[1,8,256]{2,1,0:T(8,128)(2,1)} %copy-done.26) | copy-start | bytes 12292
  404.8 19.2 %all-to-all-start.1 = ((bf16[128,2,256]{2,1,0:T(2,128)(2,1)}), bf16[128,2,256]{2,1,0:T(2,128)(2,1)S(1)}, u32[]{:S(2)}, u32[]{:S(2)}) async-start(bf16[128,2,256]{2,1,0:T(2,128)(2,1)} %broadcast_select_fusion.1), calls=%async_computation.1 | async-start | bytes 262144 | tf_op jit(solution)/shard_map/all_to_all | solution.py:212
  427.5 14.2 %all-to-all-start.2 = ((bf16[128,2,256]{2,1,0:T(2,128)(2,1)}), bf16[128,2,256]{2,1,0:T(2,128)(2,1)S(1)}, u32[]{:S(2)}, u32[]{:S(2)}) async-start(bf16[128,2,256]{2,1,0:T(2,128)(2,1)} %reshape.664), calls=%async_computation.2 | async-start | bytes 262144 | tf_op jit(solution)/shard_map/all_to_all | solution.py:265
  431.7 188.2 %all-reduce.7.cloned.1.call-start = ((), (), s32[]{:S(2)}) async-start(), calls=%async_computation.3 | async-start | bytes 5832704 | tf_op jit(solution)/shard_map/psum | solution.py:292
  (40 other events, 341.4 us)
Sparse Core Ops, SparseCore 0:
  467.8 152.0 all-reduce.6
where the time goes:
time: 644 us; the launch traced here: 634 us
  local copies, waits for them, and re-layouts  237 us (37%)
  waiting for transfers between devices  102 us (16%)
  matrix products  93.6 us (15%)
  blocking collectives  64.7 us (10%)
  starting transfers between devices  63.9 us (10%)
  other arithmetic  56.6 us (9%)
  between operations  16.1 us (3%)
    psum x1, waiting for transfers between devices, shards(): lax.psum((grad_conv, grad_time, grad_up_part, grad_kernel, grad_out), ('g...  86.6 us
    another operation x1, local copies, waits for them, and re-layouts, shards(): planes = face_planes(fine_in).reshape(bricks * 6, plane_width)  70.9 us
    psum x1, blocking collectives, shards(): lax.psum((grad_conv, grad_time, grad_up_part, grad_kernel, grad_out), ('g...  64.7 us
    dot_general x6, matrix products, shards(): jnp.einsum('oc,bcv->bov', conv_weight[tap_index], shifted[tap_index], pre...  61.1 us
    another operation x2, local copies, waits for them, and re-layouts, face_planes(): return jnp.stack(faces_list, axis=1).reshape(bricks, 6, channels * 64)  38.4 us
    unnamed x128, local copies, waits for them, and re-layouts  34.3 us
    ppermute x12, starting transfers between devices, passed_along(): return lax.ppermute(value, axis, pairs)  32.5 us
    gather x2, local copies, waits for them, and re-layouts, shards(): arrived[jnp.minimum(recv_bucket, gap_count - 1) * MFACE + jnp.minimum(ord...  13.8 us
  transfers between devices with their start and end apart: 20, of which 5 were waited for; matrix products, arithmetic and copies ran while one was open for 12% of the time, Pallas kernels for 0%

commit v1 on v0

v1 whole, which is shorter than its diff:
```python
import math

import jax
import jax.numpy as jnp
import numpy as np
from jax import lax
from jax.experimental import pallas as pl
from jax.experimental.pallas import tpu as pltpu
from jax.sharding import PartitionSpec as P

F32 = jnp.float32
BF16 = jnp.bfloat16
MESH = pl.DeviceIdType.MESH
NDEV = 128
NX = 8
NY = 16
BD = 64
CH = 64
VOX = 512
CW = 256
MFACE = 12
NBUCKET = 12
STEP = 8
TROWS = 464
GROWS = 5248
PAYLOAD = 6144
VMEM = pl.BlockSpec(memory_space=pltpu.VMEM)
SMEM = pl.BlockSpec(memory_space=pltpu.SMEM)

NN = (((1,), (0,)), ((), ()))
NT = (((1,), (1,)), ((), ()))


def mm(a, b, dims=NN):
    return lax.dot_general(a, b, dims, preferred_element_type=F32)


def sigmoid(u):
    return 0.5 * jnp.tanh(0.5 * u) + 0.5


def face_selector():
    table = np.zeros((VOX, 4 * 64), np.float32)
    for high in range(8):
        for low in range(8):
            place = 8 * high + low
            table[64 * high + 56 + low, place] = 1
            table[64 * high + low, 64 + place] = 1
            table[64 * high + 8 * low + 7, 128 + place] = 1
            table[64 * high + 8 * low, 192 + place] = 1
    return table


def face_spreader(table):
    out = np.zeros((4, 128, 2 * VOX), np.float32)
    for face in range(4):
        part = table[:, 64 * face : 64 * face + 64].T
        out[face, :64, :VOX] = part
        out[face, 64:, VOX:] = part
    return out


def bucket_offset(bucket):
    face, extra = bucket // 2, bucket % 2
    distance = 2 * (face // 2) + 1 + extra
    return distance if face % 2 == 0 else -distance


RIM_BLOCKS = (
    (0, 8, 1, 0),
    (8, 8, -1, 0),
    (16, 16, 0, 1),
    (32, 16, 0, -1),
    (48, 8, 1, 1),
    (56, 8, 1, -1),
    (64, 8, -1, 1),
    (72, 8, -1, -1),
)


def signal_all(me):
    barrier = pltpu.get_barrier_semaphore()

    def signal(step, carry):
        other = lax.rem(me + step, NDEV)
        pl.semaphore_signal(
            barrier, inc=1, device_id=(other // NY, lax.rem(other, NY)), device_id_type=MESH
        )
        return carry

    lax.fori_loop(1, NDEV, signal, 0)
    return barrier


def send_rows(me, src, dst, ssem, rsem):
    def send(step, carry):
        other = lax.rem(me + step, NDEV)
        pltpu.make_async_remote_copy(
            src_ref=src.at[pl.ds(2 * other, 2)],
            dst_ref=dst.at[pl.ds(2 * me, 2)],
            send_sem=ssem,
            recv_sem=rsem,
            device_id=(other // NY, lax.rem(other, NY)),
            device_id_type=MESH,
        ).start()
        return carry

    lax.fori_loop(1, NDEV, send, 0)
    dst[pl.ds(2 * me, 2)] = src[pl.ds(2 * me, 2)]
    other = lax.rem(me + 1, NDEV)
    every = pl.ds(0, 2 * (NDEV - 1))
    return pltpu.make_async_remote_copy(
        src_ref=src.at[every],
        dst_ref=dst.at[every],
        send_sem=ssem,
        recv_sem=rsem,
        device_id=(other // NY, lax.rem(other, NY)),
        device_id_type=MESH,
    )


def route_kernel(nb_ref, own_ref, index_ref, source_ref, slot_ref):
    me = lax.axis_index("gx") * NY + lax.axis_index("gy")
    square = jnp.concatenate(
        [nb_ref[...].astype(F32), own_ref[...].astype(F32), jnp.zeros((BD, 121), F32)], axis=1
    )
    flat = jnp.concatenate([square, square], axis=0).T.astype(jnp.int32)
    upper = lax.broadcasted_iota(jnp.int32, (BD, BD), 0)
    across = lax.broadcasted_iota(jnp.int32, (BD, BD), 1)
    earlier = upper < across
    slots = lax.broadcasted_iota(jnp.int32, (2 * MFACE, BD), 0)
    order = lax.broadcasted_iota(jnp.int32, (2 * MFACE, BD), 1)
    for face in range(6):
        facing = face + 1 - 2 * (face % 2)
        sign = 1 - 2 * (face % 2)
        row, column = flat[face : face + 1, :BD], nb_ref[:, face : face + 1]
        holder, holder_c = row >> 6, column >> 6
        local = row & 63
        present = row >= 0
        away = present & (holder != me)
        extra = ((sign * (holder - me) + NDEV) & (NDEV - 1)) - (2 * (face // 2) + 1)
        extra = jnp.clip(extra, 0, 1)
        alike = holder_c == holder
        rank_out = jnp.sum((alike & earlier).astype(jnp.int32), axis=0, keepdims=True)
        rank_in = jnp.sum((alike & (column < row)).astype(jnp.int32), axis=0, keepdims=True)
        place = jnp.where(away, extra * MFACE + jnp.minimum(rank_out, MFACE - 1), -1)
        found = jnp.sum(jnp.where(slots == place, order, 0), axis=1, keepdims=True)
        source_ref[:, face : face + 1] = found
        far = 6 * BD + facing * (2 * MFACE) + extra * MFACE + jnp.minimum(rank_in, MFACE - 1)
        near = facing * BD + local
        index_ref[face : face + 1] = jnp.where(away, far, jnp.where(present, near, 528))
    mine, mine_c = flat[6:7, :BD], own_ref[...]
    twin = jnp.sum(((mine == mine_c) & earlier).astype(jnp.int32), axis=0, keepdims=True)
    slot = mine * 2 + jnp.minimum(twin, 1)
    slot_ref[...] = jnp.concatenate([slot, jnp.full((1, BD), -1, jnp.int32)], axis=1)


def fine_kernel(
    src_ref, idx_ref, x_ref, sel_ref, spread_ref, cin_ref, cw_ref, tw_ref, basis_ref, slot_ref, cell_ref,
    fa_ref, tt_ref, rows_ref, rim_ref,
    own, planes, out_buf, rim_buf, shifted, slope, active_buf, tap_buf, near, spread, weight, pool, rows_buf,
    xsem, fsem, tsem, ssem, rsem, rows_ssem, rows_rsem,
):
    gx, gy = lax.axis_index("gx"), lax.axis_index("gy")
    me = gx * NY + gy
    loads = []
    for part in range(4):
        bricks = pl.ds(16 * part, 16)
        loads.append(
            pltpu.make_async_copy(x_ref.at[bricks], shifted.at[bricks, pl.ds(0, CH)], xsem.at[part])
        )
        loads[-1].start()
    barrier = signal_all(me)
    face_to = []
    for bucket in range(NBUCKET):
        other = lax.rem(me + bucket_offset(bucket) + NDEV, NDEV)
        face_to.append((other // NY, lax.rem(other, NY)))
    rim_to = [
        (lax.rem(gx + dx + NX, NX), lax.rem(gy + dy + NY, NY)) for _, _, dx, dy in RIM_BLOCKS
    ]

    rim = cin_ref[...].astype(F32)
    rim = (rim * sigmoid(rim)).astype(BF16).astype(F32)
    cube = rim.reshape(16, 8, CW)
    rim_buf[0:8] = cube[15]
    rim_buf[8:16] = cube[0]
    rim_buf[16:32] = cube[:, 7, :]
    rim_buf[32:48] = cube[:, 0, :]
    rim_buf[48:56] = jnp.broadcast_to(cube[15, 7:8], (8, CW))
    rim_buf[56:64] = jnp.broadcast_to(cube[15, 0:1], (8, CW))
    rim_buf[64:72] = jnp.broadcast_to(cube[0, 7:8], (8, CW))
    rim_buf[72:80] = jnp.broadcast_to(cube[0, 0:1], (8, CW))

    low = lax.broadcasted_iota(jnp.int32, (32, 128), 1) < 64

    def flip(values):
        return jnp.concatenate([values[:, 64:], values[:, :64]], axis=1)

    def pack(values, upper):
        top, bottom = values[:32], values[32:]
        if upper:
            return jnp.where(low, flip(top), bottom)
        return jnp.where(low, top, flip(bottom))

    def extract(group, carry):
        rows = shifted[pl.ds(group * 4, 4), 0:CH].reshape(4 * CH, VOX)
        picked = mm(rows, sel_ref[...]).astype(BF16)
        for b in range(4):
            n = group * 4 + b
            brick = rows[64 * b : 64 * b + 64]
            both = picked[64 * b : 64 * b + 64]
            for face, plane in enumerate(
                (
                    pack(brick[:, 384:], True),
                    pack(brick[:, :128], False),
                    pack(both[:, :128], False),
                    pack(both[:, :128], True),
                    pack(both[:, 128:], False),
                    pack(both[:, 128:], True),
                )
            ):
                own[face * BD + n] = plane
                planes[face * BD + n] = plane
        return carry

    for part in range(4):
        loads[part].wait()
        lax.fori_loop(4 * part, 4 * part + 4, extract, 0)
    planes[528:544] = jnp.zeros((16, 32, 128), BF16)

    pl.semaphore_wait(barrier, NDEV - 1)
    copies = []
    for face in range(6):

        def gather(slot, carry):
            out_buf[face * 2 * MFACE + slot] = own[face * BD + src_ref[slot, face]]
            return carry

        lax.fori_loop(0, 2 * MFACE, gather, 0)
        for bucket in (2 * face, 2 * face + 1):
            copies.append(
                pltpu.make_async_remote_copy(
                    src_ref=out_buf.at[pl.ds(bucket * MFACE, MFACE)],
                    dst_ref=planes.at[pl.ds(6 * BD + bucket * MFACE, MFACE)],
                    send_sem=ssem.at[bucket],
                    recv_sem=rsem.at[bucket],
                    device_id=face_to[bucket],
                    device_id_type=MESH,
                )
            )
            copies[-1].start()
    for number, (first, rows, _, _) in enumerate(RIM_BLOCKS):
        copies.append(
            pltpu.make_async_remote_copy(
                src_ref=rim_buf.at[pl.ds(first, rows)],
                dst_ref=rim_ref.at[pl.ds(first, rows)],
                send_sem=ssem.at[NBUCKET + number],
                recv_sem=rsem.at[NBUCKET + number],
                device_id=rim_to[number],
                device_id_type=MESH,
            )
        )
        copies[-1].start()

    weight[...] = jnp.concatenate([cw_ref[k] for k in range(7)], axis=1)
    pool[...] = jnp.zeros_like(pool)
    lane = lax.broadcasted_iota(jnp.int32, (CH, VOX), 1)
    by, bz = lane // 8 % 8, lane % 8
    keep = (by < 7, by > 0, bz < 7, bz > 0)
    tall_low = lax.broadcasted_iota(jnp.int32, (CH, 128), 1) < 64
    zero = jnp.zeros((CH, 128), BF16)

    def turned(values, shift):
        return jnp.concatenate([values[:, shift:], values[:, :shift]], axis=1)

    def shift_brick(n):
        field = shifted[n, 0:CH]
        flipped = turned(field, 64)
        shifted[n, 64:128, : VOX - 128] = flipped[:, : VOX - 128]
        shifted[n, 64:128, VOX - 128 :] = jnp.where(tall_low, flipped[:, VOX - 128 :], zero)
        back = turned(field, VOX - 64)
        shifted[n, 128:192, 128:] = back[:, 128:]
        shifted[n, 128:192, :128] = jnp.where(tall_low, zero, back[:, :128])
        for number, shift in enumerate((8, VOX - 8, 1, VOX - 1)):
            first = 192 + 64 * number
            moved = turned(field, shift)
            shifted[n, first : first + 64] = jnp.where(keep[number], moved, jnp.zeros_like(moved))
        shifted[n, 448:TROWS] = jnp.ones((16, VOX), BF16)

    def shift_two(pair, carry):
        shift_brick(2 * pair)
        shift_brick(2 * pair + 1)
        return carry

    lax.fori_loop(0, BD // 2, shift_two, 0)
    embed = jnp.sum(tw_ref[...] * basis_ref[...], axis=1, keepdims=True)
    pool_lane = lax.broadcasted_iota(jnp.int32, (CH, 128), 1)

    for copy in copies:
        copy.wait_recv()

    def fine_step(step, carry):
        for b in range(STEP):
            for face in range(6):
                near[face, 32 * b : 32 * b + 32] = planes[idx_ref[face, step * STEP + b]]
        for face in range(4):
            spread[face] = mm(near[2 + face], spread_ref[face]).astype(BF16)
        for b in range(STEP):
            n = step * STEP + b
            above, below = near[0, 32 * b : 32 * b + 32], near[1, 32 * b : 32 * b + 32]
            plus = jnp.concatenate([flip(above), above], axis=0)
            minus = jnp.concatenate([below, flip(below)], axis=0)
            shifted[n, 64:128, VOX - 128 :] += jnp.where(tall_low, zero, plus)
            shifted[n, 128:192, :128] += jnp.where(tall_low, minus, zero)
            for number in range(4):
                rows = spread[number, 32 * b : 32 * b + 32]
                first = 192 + 64 * number
                shifted[n, first : first + 32] += rows[:, :VOX]
                shifted[n, first + 32 : first + 64] += rows[:, VOX:]
            hidden = mm(weight[...], shifted[n, 0:448]) + embed
            sigma = sigmoid(hidden)
            active = hidden * sigma
            active_buf[n] = active.astype(BF16)
            mean = jnp.sum(active, axis=1, keepdims=True) * (1.0 / VOX)
            pool[0:64] += jnp.where(pool_lane == n, mean, 0.0)
            slope[n] = (sigma + active * (1.0 - sigma)).astype(BF16)
        return carry

    lax.fori_loop(0, BD // STEP, fine_step, 0)
    stored = pltpu.make_async_copy(active_buf, fa_ref, fsem)
    stored.start()

    pool[64:72] = jnp.broadcast_to(cell_ref[...], (8, 128))
    values = pool[...].astype(BF16)
    hot = (lax.broadcasted_iota(jnp.int32, (2 * NDEV, 128), 0) == slot_ref[...]).astype(BF16)
    rows_buf[...] = mm(hot, values, NT)[:, None, :]
    rows_moved = send_rows(me, rows_buf, rows_ref, rows_ssem, rows_rsem)

    def taps(pair, carry):
        first = mm(shifted[pair], slope[pair], NT)
        second = mm(shifted[pair + 32], slope[pair + 32], NT)
        tap_buf[pair] = jnp.concatenate([first, second], axis=1).astype(BF16)
        return carry

    def taps_two(step, carry):
        taps(2 * step, 0)
        taps(2 * step + 1, 0)
        return carry

    lax.fori_loop(0, 16, taps_two, 0)
    kept = pltpu.make_async_copy(tap_buf, tt_ref, tsem)
    kept.start()
    rows_moved.wait_recv()
    rows_moved.wait_send()
    for copy in copies:
        copy.wait_send()
    stored.wait()
    kept.wait()


def rim_kernel(cin_ref, rim_ref, ck_ref, ow_ref, cot_ref, base_ref, thr_ref, gouts_ref, tapt_ref, wide):
    gx, gy = lax.axis_index("gx"), lax.axis_index("gy")
    north = (gx > 0).astype(F32)
    south = (gx < NX - 1).astype(F32)
    west = (gy > 0).astype(F32)
    east = (gy < NY - 1).astype(F32)
    value = cin_ref[...].astype(F32)
    rim = value * sigmoid(value)
    rim = rim.astype(BF16).astype(F32)
    middle = jnp.concatenate([rim_ref[0:8] * north, rim, rim_ref[8:16] * south], axis=0)
    middle = middle.reshape(18, 8, CW)
    left = jnp.concatenate(
        [rim_ref[48:49] * north, rim_ref[16:32], rim_ref[64:65] * south], axis=0
    ) * west
    right = jnp.concatenate(
        [rim_ref[56:57] * north, rim_ref[32:48], rim_ref[72:73] * south], axis=0
    ) * east
    wide[0] = jnp.concatenate([left[:, None, :], middle[:, :7]], axis=1)
    wide[1] = middle
    wide[2] = jnp.concatenate([middle[:, 1:], right[:, None, :]], axis=1)
    total = value
    for p in range(3):
        for q in range(3):
            tap = wide[q, p : p + 16].reshape(128, CW)
            number = 3 * p + q
            total = total + mm(tap.astype(BF16), ck_ref[number])
            tapt_ref[number * CW : number * CW + CW] = tap.T.astype(BF16)
    base_ref[...] = total
    gouts = (cot_ref[...].astype(F32) * (1.0 / 128.0)).astype(BF16)
    gouts_ref[...] = gouts
    thr_ref[...] = mm(gouts, ow_ref[...], NT)


def reduce_kernel(
    rows_ref, base_ref, thr_ref, gouts_ref, tapt_ref, uw_ref, ow_ref, tt_any, slot_ref, out_ref, f_ref,
    payload, half, mate, got0, got1, got2, sum1, sum2, gp2, tt_ref, slot_buf, slot_got,
    csem, psem, asem, bsem, tsem, rows_ssem, rows_rsem,
):
    gx, gy = lax.axis_index("gx"), lax.axis_index("gy")
    x, c = gx // 2, lax.rem(gx, 2)
    y, z = gy // 4, lax.rem(gy, 4)
    place = (x, y, z)

    def device(axis, index):
        where = list(place)
        where[axis] = index
        return (where[0] * 2 + c, where[1] * 4 + where[2])

    peers = [
        [lax.rem(place[axis] + step, 4) for step in (1, 2, 3)] for axis in range(3)
    ]
    other_core = (x * 2 + 1 - c, gy)
    me = gx * NY + gy
    barrier = signal_all(me)
    tt_load = pltpu.make_async_copy(tt_any, tt_ref, tsem)
    tt_load.start()
    rows = rows_ref[...].reshape(2 * NDEV, 128).astype(BF16)
    pick = (lax.broadcasted_iota(jnp.int32, (8, 128), 1) == 64).astype(BF16)
    cells = mm(pick, rows, NT)[0:1].astype(jnp.int32)
    hot = lax.broadcasted_iota(jnp.int32, (128, 2 * NDEV), 0) + 1 == cells
    hot = hot.astype(BF16)
    summed = mm(hot, rows)[:, 0:CH]
    high = summed.astype(BF16)
    rest = (summed - high.astype(F32)).astype(BF16)
    uw = uw_ref[...]
    pre = base_ref[...] + mm(high, uw) + mm(rest, uw)
    sigma = sigmoid(pre)
    active = pre * sigma
    act = active.astype(BF16)
    out_ref[...] = (pre + mm(act, ow_ref[...])).astype(BF16)
    gouts = gouts_ref[...]
    gpre = gouts.astype(F32) + thr_ref[...] * (sigma + active * (1.0 - sigma))
    gpre = gpre.astype(BF16)
    gp = mm(gpre, uw, NT)
    gp = jnp.concatenate([gp, gp], axis=1).astype(BF16)
    slot_buf[...] = mm(hot.astype(F32).T.astype(BF16), gp)[:, None, :]
    for number in range(9):
        part = mm(tapt_ref[number * CW : number * CW + CW], gpre).astype(BF16)
        payload[512 * number : 512 * number + 256] = part[:, :128]
        payload[512 * number + 256 : 512 * number + 512] = part[:, 128:]
    part = mm(active.T.astype(BF16), gouts).astype(BF16)
    payload[4608:4864] = part[:, :128]
    payload[4864:5120] = part[:, 128:]
    pooled = jnp.concatenate([summed, summed], axis=1).T[0:CH]
    pooled_high = pooled.astype(BF16)
    pooled_rest = (pooled - pooled_high.astype(F32)).astype(BF16)
    part = (mm(pooled_high, gpre) + mm(pooled_rest, gpre)).astype(BF16)
    payload[5120:5184] = part[:, :128]
    payload[5184:5248] = part[:, 128:]

    pl.semaphore_wait(barrier, NDEV - 1)

    def remote(src, dst, sems, index, target):
        copy = pltpu.make_async_remote_copy(
            src_ref=src,
            dst_ref=dst,
            send_sem=sems.at[(0,) + index],
            recv_sem=sems.at[(1,) + index],
            device_id=target,
            device_id_type=MESH,
        )
        copy.start()
        return copy

    def cross(g):
        return remote(
            payload.at[pl.ds(2048 * g + (1 - c) * 1024, 1024)],
            mate.at[pl.ds(1024 * g, 1024)],
            csem, (g,), other_core,
        )

    def tap_sums():
        hot_rows = (lax.broadcasted_iota(jnp.int32, (2 * NDEV, 128), 0) == slot_ref[...]).astype(F32)
        back_rows = slot_got[...].reshape(2 * NDEV, 128).astype(BF16)
        mine = mm(hot_rows.T.astype(BF16), back_rows)
        low = lax.broadcasted_iota(jnp.int32, (32, 128), 1) < 64
        gp2[...] = jnp.where(low, mine[0:32], mine[32:64]) * (1.0 / VOX)
        for part in range(4):
            rows = 112 if part < 3 else 128

            def add(pair, total):
                scale = gp2[pl.ds(pair, 1)]
                return total + tt_ref[pair, 112 * part : 112 * part + rows].astype(F32) * scale

            total = lax.fori_loop(0, 32, add, jnp.zeros((rows, 128), F32))
            if part == 3:
                row = lax.broadcasted_iota(jnp.int32, (128, 128), 0) - 112
                total = total * jnp.where(row > 0, 1.0 + row.astype(F32) / 16.0, 1.0)
            payload[GROWS + 112 * part : GROWS + 112 * part + rows] = total.astype(BF16)
        payload[GROWS + TROWS : PAYLOAD] = jnp.zeros((PAYLOAD - GROWS - TROWS, 128), BF16)

    got = (got0, got1, got2)
    size = (256, 64, 16)
    phase = [[None] * 3 for _ in range(3)]

    def launch(p, g, src, base):
        axis = (g + p) % 3
        out = []
        for s in range(3):
            index = peers[axis][s]
            out.append(
                remote(
                    src.at[pl.ds(base + index * size[p], size[p])],
                    got[p].at[pl.ds((3 * g + s) * size[p], size[p])],
                    psem, (p, g, s), device(axis, index),
                )
            )
        return out

    def gathered(p, g, src, base):
        axis = (g + p) % 3
        for copy in phase[p][g]:
            copy.wait_recv()
        total = src[pl.ds(base + place[axis] * size[p], size[p])].astype(F32)
        for s in range(3):
            first = (3 * g + s) * size[p]
            total = total + got[p][first : first + size[p]].astype(F32)
        return total.astype(BF16)

    def crossed(g):
        core[g].wait_recv()
        half[1024 * g : 1024 * g + 1024] = (
            payload[pl.ds(2048 * g + c * 1024, 1024)].astype(F32)
            + mate[1024 * g : 1024 * g + 1024].astype(F32)
        ).astype(BF16)
        phase[0][g] = launch(0, g, half, 1024 * g)

    def first_sum(g):
        sum1[256 * g : 256 * g + 256] = gathered(0, g, half, 1024 * g)
        phase[1][g] = launch(1, g, sum1, 256 * g)

    def second_sum(g):
        sum2[64 * g : 64 * g + 64] = gathered(1, g, sum1, 256 * g)
        phase[2][g] = launch(2, g, sum2, 64 * g)

    bases = []
    for g in range(3):
        i0, i1, i2 = place[g % 3], place[(g + 1) % 3], place[(g + 2) % 3]
        start = 2048 * g + c * 1024
        bases.append((start + i0 * 256, start + i0 * 256 + i1 * 64, start + i0 * 256 + i1 * 64 + i2 * 16))
    back = [[None] * 3 for _ in range(3)]

    def spread(p, g):
        axis = (g + p) % 3
        where = f_ref.at[pl.ds(bases[g][p], size[p])]
        back[p][g] = [
            remote(where, where, asem, (p, g, s), device(axis, peers[axis][s])) for s in range(3)
        ]

    def third_sum(g):
        f_ref[pl.ds(bases[g][2], 16)] = gathered(2, g, sum2, 64 * g)
        spread(2, g)

    def onward(p, g):
        for copy in back[p + 1][g]:
            copy.wait_recv()
        spread(p, g)

    last = []

    def across(g):
        for copy in back[0][g]:
            copy.wait_recv()
        where = f_ref.at[pl.ds(2048 * g + c * 1024, 1024)]
        last.append(remote(where, where, bsem, (g,), other_core))

    core = [cross(0), cross(1)]
    rows_moved = send_rows(me, slot_buf, slot_got, rows_ssem, rows_rsem)
    crossed(0)
    crossed(1)
    tt_load.wait()
    rows_moved.wait_recv()
    tap_sums()
    core.append(cross(2))
    first_sum(0)
    first_sum(1)
    crossed(2)
    second_sum(0)
    second_sum(1)
    first_sum(2)
    third_sum(0)
    third_sum(1)
    second_sum(2)
    onward(1, 0)
    onward(1, 1)
    third_sum(2)
    onward(0, 0)
    onward(0, 1)
    onward(1, 2)
    across(0)
    across(1)
    onward(0, 2)
    across(2)
    for copy in last:
        copy.wait_recv()
    rows_moved.wait_send()
    for copy in core + last:
        copy.wait_send()
    for p in range(3):
        for g in range(3):
            for copy in phase[p][g] + back[p][g]:
                copy.wait_send()


def result_kernel(f_ref, basis_ref, fa_ref, co_ref, fa_out, co_out, conv_ref, time_ref, up_ref, kernel_ref, out_ref, sem):
    moved = pltpu.make_async_copy(fa_ref, fa_out, sem)
    moved.start()
    co_out[...] = co_ref[...]
    for number in range(9):
        kernel_ref[number, :, :128] = f_ref[512 * number : 512 * number + 256].astype(F32)
        kernel_ref[number, :, 128:] = f_ref[512 * number + 256 : 512 * number + 512].astype(F32)
    out_ref[:, :128] = f_ref[4608:4864].astype(F32)
    out_ref[:, 128:] = f_ref[4864:5120].astype(F32)
    up_ref[:, :128] = f_ref[5120:5184].astype(F32)
    up_ref[:, 128:] = f_ref[5184:5248].astype(F32)
    tail = f_ref[GROWS : GROWS + TROWS].astype(F32)
    tail = tail + jnp.concatenate([tail[:, 64:], tail[:, :64]], axis=1)
    for k in range(7):
        block = tail[64 * k : 64 * k + 64]
        conv_ref[k] = jnp.concatenate([block, block], axis=0).T[:CH, :CH]
    row = lax.broadcasted_iota(jnp.int32, (16, 128), 0).astype(F32)
    plain = jnp.sum(tail[448:464] / (1.0 + row / 16.0), axis=0, keepdims=True) / 16.0
    column = jnp.broadcast_to(plain, (128, 128)).T[:CH, 0:1]
    time_ref[...] = column * basis_ref[...]
    moved.wait()


def time_features(timestep, channels):
    half_count = channels // 2
    frequency = jnp.exp(-math.log(10000.0) * jnp.arange(half_count, dtype=jnp.float32) / half_count)
    angles = timestep[0].astype(jnp.float32) * frequency
    return jnp.concatenate([jnp.sin(angles), jnp.cos(angles)])


def shards(
    fine_in, neighbours, parent_dev, parent_cell, timestep, conv_weight, time_weight, up_weight,
    coarse_in, coarse_kernel_in, out_weight, coarse_cot,
):
    sds = jax.ShapeDtypeStruct
    anywhere = pl.BlockSpec(memory_space=pl.ANY)
    selector = face_selector()
    basis = time_features(timestep, CH)[None, :]
    cell_lane = jnp.pad(parent_cell.astype(F32) + 1.0, (0, 64))[None, :]
    cin = coarse_in.reshape(128, CW)
    cot = coarse_cot.reshape(128, CW)

    index, source, slot = pl.pallas_call(
        route_kernel,
        out_shape=(
            sds((6, BD), jnp.int32), sds((2 * MFACE, 6), jnp.int32), sds((1, 128), jnp.int32),
        ),
        in_specs=[VMEM] * 2,
        out_specs=(VMEM,) * 3,
        name="routes",
    )(neighbours, parent_dev)

    fine_act, tt, rows_in, rim = pl.pallas_call(
        fine_kernel,
        out_shape=(
            sds((BD, CH, VOX), BF16), sds((32, TROWS, 128), BF16), sds((2 * NDEV, 1, 128), F32),
            sds((80, CW), F32),
        ),
        in_specs=[SMEM, SMEM, anywhere] + [VMEM] * 8,
        out_specs=(anywhere, anywhere, VMEM, VMEM),
        scratch_shapes=[
            pltpu.VMEM((6 * BD, 32, 128), BF16),
            pltpu.VMEM((544, 32, 128), BF16),
            pltpu.VMEM((NBUCKET * MFACE, 32, 128), BF16),
            pltpu.VMEM((80, CW), F32),
            pltpu.VMEM((BD, TROWS, VOX), BF16),
            pltpu.VMEM((BD, CH, VOX), BF16),
            pltpu.VMEM((BD, CH, VOX), BF16),
            pltpu.VMEM((32, TROWS, 128), BF16),
            pltpu.VMEM((6, 32 * STEP, 128), BF16),
            pltpu.VMEM((4, 32 * STEP, 2 * VOX), BF16),
            pltpu.VMEM((CH, 448), BF16),
            pltpu.VMEM((128, 128), F32),
            pltpu.VMEM((2 * NDEV, 1, 128), F32),
            pltpu.SemaphoreType.DMA((4,)),
            pltpu.SemaphoreType.DMA,
            pltpu.SemaphoreType.DMA,
            pltpu.SemaphoreType.DMA((20,)),
            pltpu.SemaphoreType.DMA((20,)),
            pltpu.SemaphoreType.DMA,
            pltpu.SemaphoreType.DMA,
        ],
        compiler_params=pltpu.CompilerParams(
            collective_id=0, has_side_effects=True, vmem_limit_bytes=60 * 2**20
        ),
        name="fine",
    )(
        source, index, fine_in, jnp.asarray(selector, BF16), jnp.asarray(face_spreader(selector), BF16),
        cin, conv_weight, time_weight, basis, slot, cell_lane,
    )

    base, through, gouts, tapt = pl.pallas_call(
        rim_kernel,
        out_shape=(
            sds((128, CW), F32), sds((128, CW), F32), sds((128, CW), BF16), sds((9 * CW, 128), BF16),
        ),
        in_specs=[VMEM] * 5,
        out_specs=(VMEM,) * 4,
        scratch_shapes=[pltpu.VMEM((3, 18, 8, CW), F32)],
        compiler_params=pltpu.CompilerParams(vmem_limit_bytes=32 * 2**20),
        name="rim",
    )(cin, rim, coarse_kernel_in, out_weight, cot)

    coarse_out, summed = pl.pallas_call(
        reduce_kernel,
        out_shape=(sds((128, CW), BF16), sds((PAYLOAD, 128), BF16)),
        in_specs=[VMEM] * 7 + [anywhere, VMEM],
        out_specs=(VMEM, VMEM),
        scratch_shapes=[
            pltpu.VMEM((PAYLOAD, 128), BF16),
            pltpu.VMEM((3 * 1024, 128), BF16),
            pltpu.VMEM((3 * 1024, 128), BF16),
            pltpu.VMEM((9 * 256, 128), BF16),
            pltpu.VMEM((9 * 64, 128), BF16),
            pltpu.VMEM((9 * 16, 128), BF16),
            pltpu.VMEM((3 * 256, 128), BF16),
            pltpu.VMEM((3 * 64, 128), BF16),
            pltpu.VMEM((32, 128), F32),
            pltpu.VMEM((32, TROWS, 128), BF16),
            pltpu.VMEM((2 * NDEV, 1, 128), F32),
            pltpu.VMEM((2 * NDEV, 1, 128), F32),
            pltpu.SemaphoreType.DMA((2, 3)),
            pltpu.SemaphoreType.DMA((2, 3, 3, 3)),
            pltpu.SemaphoreType.DMA((2, 3, 3, 3)),
            pltpu.SemaphoreType.DMA((2, 3)),
            pltpu.SemaphoreType.DMA,
            pltpu.SemaphoreType.DMA,
            pltpu.SemaphoreType.DMA,
        ],
        compiler_params=pltpu.CompilerParams(
            collective_id=1, has_side_effects=True, vmem_limit_bytes=48 * 2**20
        ),
        name="reduce",
    )(rows_in, base, through, gouts, tapt, up_weight, out_weight, tt, slot)

    outs = pl.pallas_call(
        result_kernel,
        out_shape=(
            sds((BD, CH, VOX), BF16), sds((128, CW), BF16),
            sds((7, CH, CH), F32), sds((CH, CH), F32), sds((CH, CW), F32), sds((9, CW, CW), F32),
            sds((CW, CW), F32),
        ),
        in_specs=[VMEM, VMEM, anywhere, VMEM],
        out_specs=(anywhere,) + (VMEM,) * 6,
        scratch_shapes=[pltpu.SemaphoreType.DMA],
        compiler_params=pltpu.CompilerParams(vmem_limit_bytes=32 * 2**20),
        name="results",
    )(summed, basis, fine_act, coarse_out)
    return (outs[0], outs[1].reshape(16, 8, CW)) + tuple(outs[2:])


def solution(mesh):
    both = ("gx", "gy")
    return jax.shard_map(
        shards,
        mesh=mesh,
        in_specs=(
            P(both, None, None), P(both, None), P(both, None), P(both), P(), P(), P(), P(),
            P("gx", "gy", None), P(), P(), P("gx", "gy", None),
        ),
        out_specs=(P(both, None, None), P("gx", "gy", None), P(), P(), P(), P(), P()),
        check_vma=False,
    )
```

time: 644 us -> 123 us (0.19); the launches traced: 634 us -> 123 us
  local copies, waits for them, and re-layouts: 237 us -> 5.22 us
  Pallas kernels: 0 us -> 114 us
  waiting for transfers between devices: 102 us -> 0 us
  matrix products: 93.6 us -> 0 us
  blocking collectives: 64.7 us -> 0 us
  starting transfers between devices: 63.9 us -> 0 us
  other arithmetic: 56.6 us -> 1.3 us
  between operations: 16.1 us -> 1.55 us
    pallas_call x0 -> x5, Pallas kernels: none -> 114 us  [the longest x1 62 us: shards(): pl.pallas_call(fine_kernel, out_shape=(sds((BD, CH, VOX), BF16), sds((32,...]
    another operation x5 -> x0, local copies, waits for them, and re-layouts: 109 us -> none  [the longest x1 70.9 us: shards(): planes = face_planes(fine_in).reshape(bricks * 6, plane_width)]
    dot_general x41 -> x0, matrix products: 93.6 us -> none  [the longest x6 61.1 us: shards(): jnp.einsum('oc,bcv->bov', conv_weight[tap_index], shifted[tap_index], pre...]
    psum x1 -> x0, waiting for transfers between devices: 86.6 us -> none  [shards(): lax.psum((grad_conv, grad_time, grad_up_part, grad_kernel, grad_out), ('g...]
    psum x1 -> x0, blocking collectives: 64.7 us -> none  [shards(): lax.psum((grad_conv, grad_time, grad_up_part, grad_kernel, grad_out), ('g...]
    slice x12 -> x0, local copies, waits for them, and re-layouts: 51.3 us -> none  [the longest x1 13.4 us: shifted_list(): field[..., :voxels - 1]]
    ppermute x16 -> x0, starting transfers between devices: 43.6 us -> none  [the longest x12 32.5 us: passed_along(): return lax.ppermute(value, axis, pairs)]
    select_n x16 -> x0, other arithmetic: 40.9 us -> none  [the longest x1 10.4 us: shifted_list(): jnp.where(index_y == 0, spread_plane(nearby[:, 3], 1), jnp.concatenate([z...]
  transfers between devices with their start and end apart: 20 -> 0, of which waited for: 5 -> 0; matrix products, arithmetic and copies ran while one was open for 12% -> 0% of each run, Pallas kernels for 0% -> 0%
where the time goes in v1:
time: 123 us
  Pallas kernels  114 us (93%)
  local copies, waits for them, and re-layouts  5.22 us (4%)
  between operations  1.55 us (1%)
  other arithmetic  1.3 us (1%)
    pallas_call x1, Pallas kernels, shards(): pl.pallas_call(fine_kernel, out_shape=(sds((BD, CH, VOX), BF16), sds((32,...  62 us
    pallas_call x1, Pallas kernels, shards(): pl.pallas_call(reduce_kernel, out_shape=(sds((128, CW), BF16), sds((PAYLO...  46.5 us
    unnamed x22, local copies, waits for them, and re-layouts  4.71 us
    pallas_call x1, Pallas kernels, shards(): pl.pallas_call(result_kernel, out_shape=(sds((BD, CH, VOX), BF16), sds((1...  3.64 us

profile of v1, /device:TPU:1, one launch (start us, length us, event | category | flops | bytes accessed | tf_op | source)
XLA Modules:
  0.0 122.6 jit_solution(10351021261339198557)
XLA Ops:
  0.6 0.0 copy-start.2
  0.6 0.0 copy-start.6
  0.7 0.0 copy-start.1
  0.7 0.0 copy-start.3
  0.7 0.0 copy-start.7
  1.4 0.7 convert_add_fusion
  2.1 0.5 pad_bitcast_fusion.cell_ref
  2.7 0.6 maximum_bitcast_fusion.basis_ref
  3.3 1.4 %copy.21.nb_ref = s32[64,6]{1,0:T(8,128)} copy(s32[64,6]{0,1:T(8,128)} %param.15) | data formatting | bytes 3072 | tf_op args[1]
  4.6 1.4 %copy.22.own_ref = s32[64,1]{1,0:T(8,128)} copy(s32[64,1]{0,1:T(1,128)} %param.16) | data formatting | bytes 512 | tf_op args[2]
  6.0 1.9 %routes.1 = (s32[6,64]{1,0:T(8,128)}, s32[24,6]{1,0:T(8,128)}, s32[1,128]{1,0:T(1,128)}) custom-call(s32[64,6]{1,0:T(8,128)} %copy.21.nb_ref, s32[64,1]{1,0:T(8,128)} %copy.22.own_ref), custom_call_target="tpu_custom_call" | custom-call | tf_op jit(solution)/shard_map/routes/pallas_call | solution.py:647
  7.9 0.0 copy-start.9
  7.9 0.0 copy-start.8
  7.9 62.0 %fine.1 = (bf16[64,64,512]{2,1,0:T(8,128)(2,1)}, bf16[32,464,128]{2,1,0:T(8,128)(2,1)}, f32[256,1,128]{2,1,0:T(1,128)}, f32[80,256]{1,0:T(8,128)}) custom-call(s32[24,6]{1,0:T(8,128)} %get-tuple-element.27.src_ref, s32[6,64]{1,0:T(8,128)} %get-tuple-element.28.idx_ref, bf16[64,64,512]{2,1,0:T(8,128)(2,1)} %x_ref.1, bf16[512,256]{1,0:T(8,128)(2,1)} %constant.14.clone.sel_ref, ...), custom_call_target="tpu_custom_call" | custom-call | tf_op jit(solution)/shard_map/fine/pallas_call | solution.py:657
  70.0 0.0 copy-start
  70.0 0.0 copy-done.2
  70.0 0.0 copy-done.6
  70.0 0.0 copy-done.1
  70.0 0.0 copy-done.3
  70.0 0.0 copy-start.5
  70.0 1.0 copy-done.5
  71.0 0.4 rim.1
  71.4 0.0 copy-done.7
  71.5 0.0 copy-done.9
  71.5 0.0 copy-start.4
  71.5 0.9 copy-done.4
  72.4 46.5 %reduce.1 = (bf16[128,256]{1,0:T(8,128)(2,1)S(1)}, bf16[6144,128]{1,0:T(8,128)(2,1)S(1)}) custom-call(f32[256,1,128]{2,1,0:T(1,128)S(1)} %copy-done.4, f32[128,256]{1,0:T(8,128)S(1)} %get-tuple-element.32.base_ref, f32[128,256]{1,0:T(8,128)S(1)} %get-tuple-element.33.thr_ref, bf16[128,256]{1,0:T(8,128)(2,1)S(1)} %get-tuple-element.34.gouts_ref, ...), custom_call_target="tpu_custom_call" | custom-call | tf_op jit(solution)/shard_map/reduce/pallas_call | solution.py:708
  118.9 0.0 copy-done.8
  118.9 0.0 copy-done
  118.9 3.6 %results.1 = (bf16[64,64,512]{2,1,0:T(8,128)(2,1)}, bf16[128,256]{1,0:T(8,128)(2,1)}, f32[7,64,64]{2,1,0:T(8,128)}, f32[64,64]{1,0:T(8,128)}, f32[64,256]{1,0:T(...) custom-call(bf16[6144,128]{1,0:T(8,128)(2,1)S(1)} %get-tuple-element.37.f_ref, f32[1,64]{1,0:T(1,128)S(1)} %copy-done.8, ...), custom_call_target="tpu_custom_call" | custom-call | tf_op jit(solution)/shard_map/results/pallas_call | solution.py:740
  (1 shorter events, 0.0 us)
Async XLA Ops:
  0.6 69.3 %copy-start.2 = (bf16[256,256]{1,0:T(8,128)(2,1)S(1)}, bf16[256,256]{1,0:T(8,128)(2,1)}, u32[]{:S(2)}) copy-start(bf16[256,256]{1,0:T(8,128)(2,1)} %ow_ref.3) | copy-start | bytes 393220
  0.6 69.3 %copy-start.6 = (bf16[16,8,256]{2,1,0:T(8,128)(2,1)S(1)}, bf16[16,8,256]{2,1,0:T(8,128)(2,1)}, u32[]{:S(2)}) copy-start(bf16[16,8,256]{2,1,0:T(8,128)(2,1)} %param.25) | copy-start | bytes 196612
  0.7 69.3 %copy-start.1 = (bf16[9,256,256]{2,1,0:T(8,128)(2,1)S(1)}, bf16[9,256,256]{2,1,0:T(8,128)(2,1)}, u32[]{:S(2)}) copy-start(bf16[9,256,256]{2,1,0:T(8,128)(2,1)} %ck_ref.1) | copy-start | bytes 3538948
  0.7 69.3 %copy-start.3 = (bf16[16,8,256]{2,1,0:T(8,128)(2,1)S(1)}, bf16[16,8,256]{2,1,0:T(8,128)(2,1)}, u32[]{:S(2)}) copy-start(bf16[16,8,256]{2,1,0:T(8,128)(2,1)} %param.22) | copy-start | bytes 196612
  0.7 70.8 %copy-start.7 = (bf16[64,256]{1,0:T(8,128)(2,1)S(1)}, bf16[64,256]{1,0:T(8,128)(2,1)}, u32[]{:S(2)}) copy-start(bf16[64,256]{1,0:T(8,128)(2,1)} %uw_ref.1) | copy-start | bytes 98308
  7.9 63.5 %copy-start.9 = (s32[1,128]{1,0:T(1,128)S(1)}, s32[1,128]{1,0:T(1,128)}, u32[]{:S(2)}) copy-start(s32[1,128]{1,0:T(1,128)} %get-tuple-element.29.slot_ref) | copy-start | bytes 1540
  7.9 111.0 %copy-start.8 = (f32[1,64]{1,0:T(1,128)S(1)}, f32[1,64]{1,0:T(1,128)}, u32[]{:S(2)}) copy-start(f32[1,64]{1,0:T(1,128)} %maximum_bitcast_fusion.basis_ref) | copy-start | bytes 772
  70.0 49.0 %copy-start = (bf16[64,64,512]{2,1,0:T(8,128)(2,1)S(1)}, bf16[64,64,512]{2,1,0:T(8,128)(2,1)}, u32[]{:S(2)}) copy-start(bf16[64,64,512]{2,1,0:T(8,128)(2,1)} %get-tuple-element.38.fa_ref) | copy-start | bytes 12582916
  70.0 1.0 copy-start.5
  71.5 0.9 copy-start.4

commit v2 on v1

--- a/solution.py
+++ b/solution.py
@@ -24,6 +24,7 @@
 TROWS = 464
 GROWS = 5248
 PAYLOAD = 6144
+LATE = 512
 VMEM = pl.BlockSpec(memory_space=pltpu.VMEM)
 SMEM = pl.BlockSpec(memory_space=pltpu.SMEM)
 
@@ -78,53 +79,43 @@
 )
 
 
-def signal_all(me):
+def peers_of(gx, gy):
+    line_x = [lax.rem(gx + step, NX) for step in range(1, NX)]
+    line_y = [lax.rem(gy + step, NY) for step in range(1, NY)]
+    return [(i, (i, gy)) for i in line_x], [(i, (gx, i)) for i in line_y]
+
+
+def greet(devices):
     barrier = pltpu.get_barrier_semaphore()
-
-    def signal(step, carry):
-        other = lax.rem(me + step, NDEV)
-        pl.semaphore_signal(
-            barrier, inc=1, device_id=(other // NY, lax.rem(other, NY)), device_id_type=MESH
+    for other in devices:
+        pl.semaphore_signal(barrier, inc=1, device_id=other, device_id_type=MESH)
+    return barrier
+
+
+def send_each(peers, src_of, dst, ssem, rsem):
+    copies = []
+    for number, (index, other) in enumerate(peers):
+        copies.append(
+            pltpu.make_async_remote_copy(
+                src_ref=src_of(index),
+                dst_ref=dst,
+                send_sem=ssem.at[number],
+                recv_sem=rsem.at[number],
+                device_id=other,
+                device_id_type=MESH,
+            )
         )
-        return carry
-
-    lax.fori_loop(1, NDEV, signal, 0)
-    return barrier
-
-
-def send_rows(me, src, dst, ssem, rsem):
-    def send(step, carry):
-        other = lax.rem(me + step, NDEV)
-        pltpu.make_async_remote_copy(
-            src_ref=src.at[pl.ds(2 * other, 2)],
-            dst_ref=dst.at[pl.ds(2 * me, 2)],
-            send_sem=ssem,
-            recv_sem=rsem,
-            device_id=(other // NY, lax.rem(other, NY)),
-            device_id_type=MESH,
-        ).start()
-        return carry
-
-    lax.fori_loop(1, NDEV, send, 0)
-    dst[pl.ds(2 * me, 2)] = src[pl.ds(2 * me, 2)]
-    other = lax.rem(me + 1, NDEV)
-    every = pl.ds(0, 2 * (NDEV - 1))
-    return pltpu.make_async_remote_copy(
-        src_ref=src.at[every],
-        dst_ref=dst.at[every],
-        send_sem=ssem,
-        recv_sem=rsem,
-        device_id=(other // NY, lax.rem(other, NY)),
-        device_id_type=MESH,
-    )
-
-
-def route_kernel(nb_ref, own_ref, index_ref, source_ref, slot_ref):
+        copies[-1].start()
+    return copies
+
+
+def route_kernel(nb_ref, own_ref, cell_in_ref, index_ref, source_ref, slot_ref, cell_ref):
     me = lax.axis_index("gx") * NY + lax.axis_index("gy")
-    square = jnp.concatenate(
-        [nb_ref[...].astype(F32), own_ref[...].astype(F32), jnp.zeros((BD, 121), F32)], axis=1
-    )
-    flat = jnp.concatenate([square, square], axis=0).T.astype(jnp.int32)
+    flat = jnp.concatenate([nb_ref[...], own_ref[...]], axis=0)
+    tall = jnp.concatenate([flat.astype(F32), jnp.zeros((121, BD), F32)], axis=0)
+    tall = jnp.concatenate([tall, tall], axis=1).T.astype(jnp.int32)
+    blank = jnp.zeros((1, BD), F32)
+    cell_ref[...] = jnp.concatenate([cell_in_ref[...].astype(F32) + 1.0, blank], axis=1)
     upper = lax.broadcasted_iota(jnp.int32, (BD, BD), 0)
     across = lax.broadcasted_iota(jnp.int32, (BD, BD), 1)
     earlier = upper < across
@@ -133,7 +124,7 @@
     for face in range(6):
         facing = face + 1 - 2 * (face % 2)
         sign = 1 - 2 * (face % 2)
-        row, column = flat[face : face + 1, :BD], nb_ref[:, face : face + 1]
+        row, column = flat[face : face + 1], tall[:BD, face : face + 1]
         holder, holder_c = row >> 6, column >> 6
         local = row & 63
         present = row >= 0
@@ -149,17 +140,17 @@
         far = 6 * BD + facing * (2 * MFACE) + extra * MFACE + jnp.minimum(rank_in, MFACE - 1)
         near = facing * BD + local
         index_ref[face : face + 1] = jnp.where(away, far, jnp.where(present, near, 528))
-    mine, mine_c = flat[6:7, :BD], own_ref[...]
+    mine, mine_c = flat[6:7], tall[:BD, 6:7]
     twin = jnp.sum(((mine == mine_c) & earlier).astype(jnp.int32), axis=0, keepdims=True)
-    slot = mine * 2 + jnp.minimum(twin, 1)
+    slot = ((mine & 15) * 8 + (mine >> 4)) * 2 + jnp.minimum(twin, 1)
     slot_ref[...] = jnp.concatenate([slot, jnp.full((1, BD), -1, jnp.int32)], axis=1)
 
 
 def fine_kernel(
     src_ref, idx_ref, x_ref, sel_ref, spread_ref, cin_ref, cw_ref, tw_ref, basis_ref, slot_ref, cell_ref,
     fa_ref, tt_ref, rows_ref, rim_ref,
-    own, planes, out_buf, rim_buf, shifted, slope, active_buf, tap_buf, near, spread, weight, pool, rows_buf,
-    xsem, fsem, tsem, ssem, rsem, rows_ssem, rows_rsem,
+    own, planes, out_buf, rim_buf, shifted, slope, active_buf, tap_buf, near, spread, weight, pool, rows_buf, rows_mid,
+    xsem, fsem, tsem, ssem, rsem, ysend, yrecv, xsend, xrecv,
 ):
     gx, gy = lax.axis_index("gx"), lax.axis_index("gy")
     me = gx * NY + gy
@@ -170,7 +161,6 @@
             pltpu.make_async_copy(x_ref.at[bricks], shifted.at[bricks, pl.ds(0, CH)], xsem.at[part])
         )
         loads[-1].start()
-    barrier = signal_all(me)
     face_to = []
     for bucket in range(NBUCKET):
         other = lax.rem(me + bucket_offset(bucket) + NDEV, NDEV)
@@ -178,6 +168,10 @@
     rim_to = [
         (lax.rem(gx + dx + NX, NX), lax.rem(gy + dy + NY, NY)) for _, _, dx, dy in RIM_BLOCKS
     ]
+
+    peers_x, peers_y = peers_of(gx, gy)
+    partners = face_to + rim_to + [other for _, other in peers_x + peers_y]
+    barrier = greet(partners)
 
     rim = cin_ref[...].astype(F32)
     rim = (rim * sigmoid(rim)).astype(BF16).astype(F32)
@@ -228,7 +222,7 @@
         lax.fori_loop(4 * part, 4 * part + 4, extract, 0)
     planes[528:544] = jnp.zeros((16, 32, 128), BF16)
 
-    pl.semaphore_wait(barrier, NDEV - 1)
+    pl.semaphore_wait(barrier, len(partners))
     copies = []
     for face in range(6):
 
@@ -333,8 +327,9 @@
     pool[64:72] = jnp.broadcast_to(cell_ref[...], (8, 128))
     values = pool[...].astype(BF16)
     hot = (lax.broadcasted_iota(jnp.int32, (2 * NDEV, 128), 0) == slot_ref[...]).astype(BF16)
-    rows_buf[...] = mm(hot, values, NT)[:, None, :]
-    rows_moved = send_rows(me, rows_buf, rows_ref, rows_ssem, rows_rsem)
+    rows_buf[...] = mm(hot, values, NT)[:, None, :].reshape(NY, 2 * NX, 1, 128)
+    along_y = send_each(peers_y, lambda i: rows_buf.at[i], rows_mid.at[gy], ysend, yrecv)
+    rows_mid[gy] = rows_buf[gy]
 
     def taps(pair, carry):
         first = mm(shifted[pair], slope[pair], NT)
@@ -347,11 +342,20 @@
         taps(2 * step + 1, 0)
         return carry
 
-    lax.fori_loop(0, 16, taps_two, 0)
+    lax.fori_loop(0, 4, taps_two, 0)
+    for copy in along_y:
+        copy.wait_recv()
+    along_x = send_each(
+        peers_x, lambda i: rows_mid.at[:, pl.ds(2 * i, 2)], rows_ref.at[gx], xsend, xrecv
+    )
+    rows_ref[gx] = rows_mid[:, pl.ds(2 * gx, 2)]
+    lax.fori_loop(4, 16, taps_two, 0)
     kept = pltpu.make_async_copy(tap_buf, tt_ref, tsem)
     kept.start()
-    rows_moved.wait_recv()
-    rows_moved.wait_send()
+    for copy in along_x:
+        copy.wait_recv()
+    for copy in along_x + along_y:
+        copy.wait_send()
     for copy in copies:
         copy.wait_send()
     stored.wait()
@@ -393,8 +397,8 @@
 
 def reduce_kernel(
     rows_ref, base_ref, thr_ref, gouts_ref, tapt_ref, uw_ref, ow_ref, tt_any, slot_ref, out_ref, f_ref,
-    payload, half, mate, got0, got1, got2, sum1, sum2, gp2, tt_ref, slot_buf, slot_got,
-    csem, psem, asem, bsem, tsem, rows_ssem, rows_rsem,
+    payload, half, mate, got0, got1, got2, sum1, sum2, gp2, tt_ref, slot_buf, slot_mid, slot_got,
+    late, late_got, late_sum, late_all, csem, psem, asem, bsem, tsem, xsend, xrecv, ysend, yrecv, lsem, lxsem, lysem,
 ):
     gx, gy = lax.axis_index("gx"), lax.axis_index("gy")
     x, c = gx // 2, lax.rem(gx, 2)
@@ -410,8 +414,8 @@
         [lax.rem(place[axis] + step, 4) for step in (1, 2, 3)] for axis in range(3)
     ]
     other_core = (x * 2 + 1 - c, gy)
-    me = gx * NY + gy
-    barrier = signal_all(me)
+    peers_x, peers_y = peers_of(gx, gy)
+    barrier = greet([other for _, other in peers_x + peers_y])
     tt_load = pltpu.make_async_copy(tt_any, tt_ref, tsem)
     tt_load.start()
     rows = rows_ref[...].reshape(2 * NDEV, 128).astype(BF16)
@@ -433,7 +437,7 @@
     gpre = gpre.astype(BF16)
     gp = mm(gpre, uw, NT)
     gp = jnp.concatenate([gp, gp], axis=1).astype(BF16)
-    slot_buf[...] = mm(hot.astype(F32).T.astype(BF16), gp)[:, None, :]
+    slot_buf[...] = mm(hot.astype(F32).T.astype(BF16), gp)[:, None, :].reshape(NX, 2 * NY, 1, 128)
     for number in range(9):
         part = mm(tapt_ref[number * CW : number * CW + CW], gpre).astype(BF16)
         payload[512 * number : 512 * number + 256] = part[:, :128]
@@ -448,7 +452,9 @@
     payload[5120:5184] = part[:, :128]
     payload[5184:5248] = part[:, 128:]
 
-    pl.semaphore_wait(barrier, NDEV - 1)
+    payload[GROWS:PAYLOAD] = jnp.zeros((PAYLOAD - GROWS, 128), BF16)
+
+    pl.semaphore_wait(barrier, len(peers_x + peers_y))
 
     def remote(src, dst, sems, index, target):
         copy = pltpu.make_async_remote_copy(
@@ -486,8 +492,8 @@
             if part == 3:
                 row = lax.broadcasted_iota(jnp.int32, (128, 128), 0) - 112
                 total = total * jnp.where(row > 0, 1.0 + row.astype(F32) / 16.0, 1.0)
-            payload[GROWS + 112 * part : GROWS + 112 * part + rows] = total.astype(BF16)
-        payload[GROWS + TROWS : PAYLOAD] = jnp.zeros((PAYLOAD - GROWS - TROWS, 128), BF16)
+            late[112 * part : 112 * part + rows] = total.astype(BF16)
+        late[TROWS:LATE] = jnp.zeros((LATE - TROWS, 128), BF16)
 
     got = (got0, got1, got2)
     size = (256, 64, 16)
@@ -564,37 +570,55 @@
         where = f_ref.at[pl.ds(2048 * g + c * 1024, 1024)]
         last.append(remote(where, where, bsem, (g,), other_core))
 
-    core = [cross(0), cross(1)]
-    rows_moved = send_rows(me, slot_buf, slot_got, rows_ssem, rows_rsem)
-    crossed(0)
-    crossed(1)
+    back_x = send_each(peers_x, lambda i: slot_buf.at[i], slot_mid.at[gx], xsend, xrecv)
+    slot_mid[gx] = slot_buf[gx]
+    core = [cross(g) for g in range(3)]
+    for copy in back_x:
+        copy.wait_recv()
+    back_y = send_each(
+        peers_y, lambda i: slot_mid.at[:, pl.ds(2 * i, 2)], slot_got.at[gy], ysend, yrecv
+    )
+    slot_got[gy] = slot_mid[:, pl.ds(2 * gy, 2)]
+    for g in range(3):
+        crossed(g)
     tt_load.wait()
-    rows_moved.wait_recv()
+    for copy in back_y:
+        copy.wait_recv()
     tap_sums()
-    core.append(cross(2))
-    first_sum(0)
-    first_sum(1)
-    crossed(2)
-    second_sum(0)
-    second_sum(1)
-    first_sum(2)
-    third_sum(0)
-    third_sum(1)
-    second_sum(2)
-    onward(1, 0)
-    onward(1, 1)
-    third_sum(2)
-    onward(0, 0)
-    onward(0, 1)
-    onward(1, 2)
-    across(0)
-    across(1)
-    onward(0, 2)
-    across(2)
-    for copy in last:
+    late_y = send_each(
+        peers_y, lambda i: late.at[pl.ds(32 * i, 32)], late_got.at[gy], lsem.at[0], lsem.at[1]
+    )
+    late_got[gy] = late[pl.ds(pl.multiple_of(32 * gy, 32), 32)]
+    for g in range(3):
+        first_sum(g)
+    for copy in late_y:
         copy.wait_recv()
-    rows_moved.wait_send()
-    for copy in core + last:
+    total = late_got[0].astype(F32)
+    for i in range(1, NY):
+        total = total + late_got[i].astype(F32)
+    late_sum[...] = total.astype(BF16)
+    late_x = send_each(peers_x, lambda i: late_sum, late_all.at[gx], lxsem.at[0], lxsem.at[1])
+    late_all[gx] = late_sum[...]
+    for g in range(3):
+        second_sum(g)
+    for copy in late_x:
+        copy.wait_recv()
+    total = late_all[0].astype(F32)
+    for i in range(1, NX):
+        total = total + late_all[i].astype(F32)
+    where = f_ref.at[pl.ds(pl.multiple_of(PAYLOAD + 32 * gy, 32), 32)]
+    where[...] = total.astype(BF16)
+    late_back = send_each(peers_y, lambda i: where, where, lysem.at[0], lysem.at[1])
+    for g in range(3):
+        third_sum(g)
+    for p in (1, 0):
+        for g in range(3):
+            onward(p, g)
+    for g in range(3):
+        across(g)
+    for copy in last + late_back:
+        copy.wait_recv()
+    for copy in core + last + back_x + back_y + late_y + late_x + late_back:
         copy.wait_send()
     for p in range(3):
         for g in range(3):
@@ -613,7 +637,7 @@
     out_ref[:, 128:] = f_ref[4864:5120].astype(F32)
     up_ref[:, :128] = f_ref[5120:5184].astype(F32)
     up_ref[:, 128:] = f_ref[5184:5248].astype(F32)
-    tail = f_ref[GROWS : GROWS + TROWS].astype(F32)
+    tail = f_ref[PAYLOAD : PAYLOAD + TROWS].astype(F32)
     tail = tail + jnp.concatenate([tail[:, 64:], tail[:, :64]], axis=1)
     for k in range(7):
         block = tail[64 * k : 64 * k + 64]
@@ -640,24 +664,24 @@
     anywhere = pl.BlockSpec(memory_space=pl.ANY)
     selector = face_selector()
     basis = time_features(timestep, CH)[None, :]
-    cell_lane = jnp.pad(parent_cell.astype(F32) + 1.0, (0, 64))[None, :]
     cin = coarse_in.reshape(128, CW)
     cot = coarse_cot.reshape(128, CW)
 
-    index, source, slot = pl.pallas_call(
+    index, source, slot, cell_lane = pl.pallas_call(
         route_kernel,
         out_shape=(
             sds((6, BD), jnp.int32), sds((2 * MFACE, 6), jnp.int32), sds((1, 128), jnp.int32),
+            sds((1, 128), F32),
         ),
-        in_specs=[VMEM] * 2,
-        out_specs=(VMEM,) * 3,
+        in_specs=[VMEM] * 3,
+        out_specs=(VMEM,) * 4,
         name="routes",
-    )(neighbours, parent_dev)
+    )(neighbours.T, parent_dev.T, parent_cell[None, :])
 
     fine_act, tt, rows_in, rim = pl.pallas_call(
         fine_kernel,
         out_shape=(
-            sds((BD, CH, VOX), BF16), sds((32, TROWS, 128), BF16), sds((2 * NDEV, 1, 128), F32),
+            sds((BD, CH, VOX), BF16), sds((32, TROWS, 128), BF16), sds((NX, NY, 2, 1, 128), F32),
             sds((80, CW), F32),
         ),
         in_specs=[SMEM, SMEM, anywhere] + [VMEM] * 8,
@@ -675,17 +699,20 @@
             pltpu.VMEM((4, 32 * STEP, 2 * VOX), BF16),
             pltpu.VMEM((CH, 448), BF16),
             pltpu.VMEM((128, 128), F32),
-            pltpu.VMEM((2 * NDEV, 1, 128), F32),
+            pltpu.VMEM((NY, 2 * NX, 1, 128), F32),
+            pltpu.VMEM((NY, 2 * NX, 1, 128), F32),
             pltpu.SemaphoreType.DMA((4,)),
             pltpu.SemaphoreType.DMA,
             pltpu.SemaphoreType.DMA,
             pltpu.SemaphoreType.DMA((20,)),
             pltpu.SemaphoreType.DMA((20,)),
-            pltpu.SemaphoreType.DMA,
-            pltpu.SemaphoreType.DMA,
+            pltpu.SemaphoreType.DMA((NY - 1,)),
+            pltpu.SemaphoreType.DMA((NY - 1,)),
+            pltpu.SemaphoreType.DMA((NX - 1,)),
+            pltpu.SemaphoreType.DMA((NX - 1,)),
         ],
         compiler_params=pltpu.CompilerParams(
-            collective_id=0, has_side_effects=True, vmem_limit_bytes=60 * 2**20
+            collective_id=0, has_side_effects=True, vmem_limit_bytes=55 * 2**20
         ),
         name="fine",
     )(
@@ -707,7 +734,7 @@
 
     coarse_out, summed = pl.pallas_call(
         reduce_kernel,
-        out_shape=(sds((128, CW), BF16), sds((PAYLOAD, 128), BF16)),
+        out_shape=(sds((128, CW), BF16), sds((PAYLOAD + LATE, 128), BF16)),
         in_specs=[VMEM] * 7 + [anywhere, VMEM],
         out_specs=(VMEM, VMEM),
         scratch_shapes=[
@@ -721,21 +748,31 @@
             pltpu.VMEM((3 * 64, 128), BF16),
             pltpu.VMEM((32, 128), F32),
             pltpu.VMEM((32, TROWS, 128), BF16),
-            pltpu.VMEM((2 * NDEV, 1, 128), F32),
-            pltpu.VMEM((2 * NDEV, 1, 128), F32),
+            pltpu.VMEM((NX, 2 * NY, 1, 128), F32),
+            pltpu.VMEM((NX, 2 * NY, 1, 128), F32),
+            pltpu.VMEM((NY, NX, 2, 1, 128), F32),
+            pltpu.VMEM((LATE, 128), BF16),
+            pltpu.VMEM((NY, 32, 128), BF16),
+            pltpu.VMEM((32, 128), BF16),
+            pltpu.VMEM((NX, 32, 128), BF16),
             pltpu.SemaphoreType.DMA((2, 3)),
             pltpu.SemaphoreType.DMA((2, 3, 3, 3)),
             pltpu.SemaphoreType.DMA((2, 3, 3, 3)),
             pltpu.SemaphoreType.DMA((2, 3)),
             pltpu.SemaphoreType.DMA,
-            pltpu.SemaphoreType.DMA,
-            pltpu.SemaphoreType.DMA,
+            pltpu.SemaphoreType.DMA((NX - 1,)),
+            pltpu.SemaphoreType.DMA((NX - 1,)),
+            pltpu.SemaphoreType.DMA((NY - 1,)),
+            pltpu.SemaphoreType.DMA((NY - 1,)),
+            pltpu.SemaphoreType.DMA((2, NY - 1)),
+            pltpu.SemaphoreType.DMA((2, NX - 1)),
+            pltpu.SemaphoreType.DMA((2, NY - 1)),
         ],
         compiler_params=pltpu.CompilerParams(
             collective_id=1, has_side_effects=True, vmem_limit_bytes=48 * 2**20
         ),
         name="reduce",
-    )(rows_in, base, through, gouts, tapt, up_weight, out_weight, tt, slot)
+    )(rows_in.reshape(2 * NDEV, 1, 128), base, through, gouts, tapt, up_weight, out_weight, tt, slot)
 
     outs = pl.pallas_call(
         result_kernel,

time: 123 us -> 113 us (0.919)
  Pallas kernels: 114 us -> 109 us
  local copies, waits for them, and re-layouts: 5.22 us -> 1.96 us
    pallas_call x1, Pallas kernels: 46.5 us -> 43.6 us  [shards(): pl.pallas_call(reduce_kernel, out_shape=(sds((128, CW), BF16), sds((PAYLO...]
    pallas_call x1, Pallas kernels: 62 us -> 59.2 us  [shards(): pl.pallas_call(fine_kernel, out_shape=(sds((BD, CH, VOX), BF16), sds((32,...]
    unnamed x22 -> x20, local copies, waits for them, and re-layouts: 4.71 us -> 1.96 us
where the time goes in v2:
time: 113 us
  Pallas kernels  109 us (96%)
  local copies, waits for them, and re-layouts  1.96 us (2%)
  between operations  1.54 us (1%)
    pallas_call x1, Pallas kernels, shards(): pl.pallas_call(fine_kernel, out_shape=(sds((BD, CH, VOX), BF16), sds((32,...  59.2 us
    pallas_call x1, Pallas kernels, shards(): pl.pallas_call(reduce_kernel, out_shape=(sds((128, CW), BF16), sds((PAYLO...  43.6 us
    pallas_call x1, Pallas kernels, shards(): pl.pallas_call(result_kernel, out_shape=(sds((BD, CH, VOX), BF16), sds((1...  3.64 us

profile of v2, /device:TPU:1, one launch (start us, length us, event | category | flops | bytes accessed | tf_op | source)
XLA Modules:
  0.0 112.8 jit_solution(1186900551983463270)
XLA Ops:
  0.6 0.0 copy-start.2
  0.6 0.0 copy-start.6
  0.7 0.0 copy-start.1
  0.7 0.0 copy-start.3
  0.7 0.0 copy-start.7
  1.5 0.6 maximum_bitcast_fusion.basis_ref
  2.1 1.9 %routes.1 = (s32[6,64]{1,0:T(8,128)}, s32[24,6]{1,0:T(8,128)}, s32[1,128]{1,0:T(1,128)}, f32[1,128]{1,0:T(1,128)}) custom-call(s32[6,64]{1,0:T(8,128)} %bitcast.14, s32[1,64]{1,0:T(1,128)} %bitcast.15, s32[1,64]{1,0:T(1,128)} %bitcast.16), custom_call_target="tpu_custom_call" | custom-call | tf_op jit(solution)/shard_map/routes/pallas_call | solution.py:670
  3.9 0.0 copy-start.9
  3.9 0.0 copy-start.8
  3.9 59.2 %fine.1 = (bf16[64,64,512]{2,1,0:T(8,128)(2,1)}, bf16[32,464,128]{2,1,0:T(8,128)(2,1)}, f32[8,16,2,1,128]{4,3,2,1,0:T(1,128)}, f32[80,256]{1,0:T(8,128)}) custom-call(s32[24,6]{1,0:T(8,128)} %get-tuple-element.28.src_ref, s32[6,64]{1,0:T(8,128)} %get-tuple-element.29.idx_ref, bf16[64,64,512]{2,1,0:T(8,128)(2,1)} %x_ref.1, ...), custom_call_target="tpu_custom_call" | custom-call | tf_op jit(solution)/shard_map/fine/pallas_call | solution.py:681
  63.1 0.0 copy-start
  63.2 0.0 copy-done.2
  63.2 0.0 copy-done.6
  63.2 0.0 copy-done.1
  63.2 0.0 copy-done.3
  63.2 0.0 copy-start.5
  63.2 1.0 copy-done.5
  64.2 0.4 rim.1
  64.6 0.0 copy-done.7
  64.6 0.0 copy-done.9
  64.7 0.0 copy-start.4
  64.7 0.9 copy-done.4
  65.6 43.6 %reduce.1 = (bf16[128,256]{1,0:T(8,128)(2,1)S(1)}, bf16[6656,128]{1,0:T(8,128)(2,1)S(1)}) custom-call(f32[256,1,128]{2,1,0:T(1,128)S(1)} %bitcast.12, f32[128,256]{1,0:T(8,128)S(1)} %get-tuple-element.34.base_ref, f32[128,256]{1,0:T(8,128)S(1)} %get-tuple-element.35.thr_ref, bf16[128,256]{1,0:T(8,128)(2,1)S(1)} %get-tuple-element.36.gouts_ref, ...), custom_call_target="tpu_custom_call" | custom-call | tf_op jit(solution)/shard_map/reduce/pallas_call | solution.py:735
  109.2 0.0 copy-done.8
  109.2 0.0 copy-done
  109.2 3.6 %results.1 = (bf16[64,64,512]{2,1,0:T(8,128)(2,1)}, bf16[128,256]{1,0:T(8,128)(2,1)}, f32[7,64,64]{2,1,0:T(8,128)}, f32[64,64]{1,0:T(8,128)}, f32[64,256]{1,0:T(...) custom-call(bf16[6656,128]{1,0:T(8,128)(2,1)S(1)} %get-tuple-element.39.f_ref, f32[1,64]{1,0:T(1,128)S(1)} %copy-done.8, ...), custom_call_target="tpu_custom_call" | custom-call | tf_op jit(solution)/shard_map/results/pallas_call | solution.py:777
  (1 shorter events, 0.0 us)
Async XLA Ops:
  0.6 62.5 %copy-start.2 = (bf16[256,256]{1,0:T(8,128)(2,1)S(1)}, bf16[256,256]{1,0:T(8,128)(2,1)}, u32[]{:S(2)}) copy-start(bf16[256,256]{1,0:T(8,128)(2,1)} %ow_ref.3) | copy-start | bytes 393220
  0.6 62.5 %copy-start.6 = (bf16[16,8,256]{2,1,0:T(8,128)(2,1)S(1)}, bf16[16,8,256]{2,1,0:T(8,128)(2,1)}, u32[]{:S(2)}) copy-start(bf16[16,8,256]{2,1,0:T(8,128)(2,1)} %param.25) | copy-start | bytes 196612
  0.7 62.5 %copy-start.1 = (bf16[9,256,256]{2,1,0:T(8,128)(2,1)S(1)}, bf16[9,256,256]{2,1,0:T(8,128)(2,1)}, u32[]{:S(2)}) copy-start(bf16[9,256,256]{2,1,0:T(8,128)(2,1)} %ck_ref.1) | copy-start | bytes 3538948
  0.7 62.5 %copy-start.3 = (bf16[16,8,256]{2,1,0:T(8,128)(2,1)S(1)}, bf16[16,8,256]{2,1,0:T(8,128)(2,1)}, u32[]{:S(2)}) copy-start(bf16[16,8,256]{2,1,0:T(8,128)(2,1)} %param.22) | copy-start | bytes 196612
  0.7 64.0 %copy-start.7 = (bf16[64,256]{1,0:T(8,128)(2,1)S(1)}, bf16[64,256]{1,0:T(8,128)(2,1)}, u32[]{:S(2)}) copy-start(bf16[64,256]{1,0:T(8,128)(2,1)} %uw_ref.1) | copy-start | bytes 98308
  3.9 60.7 %copy-start.9 = (s32[1,128]{1,0:T(1,128)S(1)}, s32[1,128]{1,0:T(1,128)}, u32[]{:S(2)}) copy-start(s32[1,128]{1,0:T(1,128)} %get-tuple-element.30.slot_ref) | copy-start | bytes 1540
  3.9 105.2 %copy-start.8 = (f32[1,64]{1,0:T(1,128)S(1)}, f32[1,64]{1,0:T(1,128)}, u32[]{:S(2)}) copy-start(f32[1,64]{1,0:T(1,128)} %maximum_bitcast_fusion.basis_ref) | copy-start | bytes 772
  63.1 46.1 %copy-start = (bf16[64,64,512]{2,1,0:T(8,128)(2,1)S(1)}, bf16[64,64,512]{2,1,0:T(8,128)(2,1)}, u32[]{:S(2)}) copy-start(bf16[64,64,512]{2,1,0:T(8,128)(2,1)} %get-tuple-element.40.fa_ref) | copy-start | bytes 12582916
  63.2 1.0 copy-start.5
  64.7 0.9 copy-start.4

commit v3 on v2

v3 whole, which is shorter than its diff:
```python
import math

import jax
import jax.numpy as jnp
import numpy as np
from jax import lax
from jax.experimental import pallas as pl
from jax.experimental.pallas import tpu as pltpu
from jax.sharding import PartitionSpec as P

F32 = jnp.float32
BF16 = jnp.bfloat16
MESH = pl.DeviceIdType.MESH
NDEV = 128
NX = 8
NY = 16
BD = 64
CH = 64
VOX = 512
CW = 256
MFACE = 12
NBUCKET = 12
STEP = 8
TROWS = 464
GROWS = 5248
PAYLOAD = 6144
LATE = 512
VMEM = pl.BlockSpec(memory_space=pltpu.VMEM)
SMEM = pl.BlockSpec(memory_space=pltpu.SMEM)

NN = (((1,), (0,)), ((), ()))
NT = (((1,), (1,)), ((), ()))


def mm(a, b, dims=NN):
    return lax.dot_general(a, b, dims, preferred_element_type=F32)


def sigmoid(u):
    return 0.5 * jnp.tanh(0.5 * u) + 0.5


def face_selector():
    table = np.zeros((VOX, 4 * 64), np.float32)
    for high in range(8):
        for low in range(8):
            place = 8 * high + low
            table[64 * high + 56 + low, place] = 1
            table[64 * high + low, 64 + place] = 1
            table[64 * high + 8 * low + 7, 128 + place] = 1
            table[64 * high + 8 * low, 192 + place] = 1
    return table


def face_spreader(table):
    out = np.zeros((4, 128, 2 * VOX), np.float32)
    for face in range(4):
        part = table[:, 64 * face : 64 * face + 64].T
        out[face, :64, :VOX] = part
        out[face, 64:, VOX:] = part
    return out


def bucket_offset(bucket):
    face, extra = bucket // 2, bucket % 2
    distance = 2 * (face // 2) + 1 + extra
    return distance if face % 2 == 0 else -distance


RIM_BLOCKS = (
    (0, 8, 1, 0),
    (8, 8, -1, 0),
    (16, 16, 0, 1),
    (32, 16, 0, -1),
    (48, 8, 1, 1),
    (56, 8, 1, -1),
    (64, 8, -1, 1),
    (72, 8, -1, -1),
)


def peers_of(gx, gy):
    line_x = [lax.rem(gx + step, NX) for step in range(1, NX)]
    line_y = [lax.rem(gy + step, NY) for step in range(1, NY)]
    return [(i, (i, gy)) for i in line_x], [(i, (gx, i)) for i in line_y]


def greet(devices):
    barrier = pltpu.get_barrier_semaphore()
    for other in devices:
        pl.semaphore_signal(barrier, inc=1, device_id=other, device_id_type=MESH)
    return barrier


def send_each(peers, src_of, dst, ssem, rsem):
    copies = []
    for number, (index, other) in enumerate(peers):
        copies.append(
            pltpu.make_async_remote_copy(
                src_ref=src_of(index),
                dst_ref=dst,
                send_sem=ssem.at[number],
                recv_sem=rsem.at[number],
                device_id=other,
                device_id_type=MESH,
            )
        )
        copies[-1].start()
    return copies


def route_kernel(nb_ref, own_ref, cell_in_ref, index_ref, source_ref, slot_ref, cell_ref):
    me = lax.axis_index("gx") * NY + lax.axis_index("gy")
    flat = jnp.concatenate([nb_ref[...], own_ref[...]], axis=0)
    tall = jnp.concatenate([flat.astype(F32), jnp.zeros((121, BD), F32)], axis=0)
    tall = jnp.concatenate([tall, tall], axis=1).T.astype(jnp.int32)
    blank = jnp.zeros((1, BD), F32)
    cell_ref[...] = jnp.concatenate([cell_in_ref[...].astype(F32) + 1.0, blank], axis=1)
    upper = lax.broadcasted_iota(jnp.int32, (BD, BD), 0)
    across = lax.broadcasted_iota(jnp.int32, (BD, BD), 1)
    earlier = upper < across
    slots = lax.broadcasted_iota(jnp.int32, (2 * MFACE, BD), 0)
    order = lax.broadcasted_iota(jnp.int32, (2 * MFACE, BD), 1)
    for face in range(6):
        facing = face + 1 - 2 * (face % 2)
        sign = 1 - 2 * (face % 2)
        row, column = flat[face : face + 1], tall[:BD, face : face + 1]
        holder, holder_c = row >> 6, column >> 6
        local = row & 63
        present = row >= 0
        away = present & (holder != me)
        extra = ((sign * (holder - me) + NDEV) & (NDEV - 1)) - (2 * (face // 2) + 1)
        extra = jnp.clip(extra, 0, 1)
        alike = holder_c == holder
        rank_out = jnp.sum((alike & earlier).astype(jnp.int32), axis=0, keepdims=True)
        rank_in = jnp.sum((alike & (column < row)).astype(jnp.int32), axis=0, keepdims=True)
        place = jnp.where(away, extra * MFACE + jnp.minimum(rank_out, MFACE - 1), -1)
        found = jnp.sum(jnp.where(slots == place, order, 0), axis=1, keepdims=True)
        source_ref[:, face : face + 1] = found
        far = 6 * BD + facing * (2 * MFACE) + extra * MFACE + jnp.minimum(rank_in, MFACE - 1)
        near = facing * BD + local
        index_ref[face : face + 1] = jnp.where(away, far, jnp.where(present, near, 528))
    mine, mine_c = flat[6:7], tall[:BD, 6:7]
    twin = jnp.sum(((mine == mine_c) & earlier).astype(jnp.int32), axis=0, keepdims=True)
    slot = ((mine & 15) * 8 + (mine >> 4)) * 2 + jnp.minimum(twin, 1)
    slot_ref[...] = jnp.concatenate([slot, jnp.full((1, BD), -1, jnp.int32)], axis=1)


def rim_pass(gx, gy, cin_ref, rim_ref, ck_ref, ow_ref, cot_ref, base_ref, thr_ref, gouts_ref, tapt_ref, wide):
    north = (gx > 0).astype(F32)
    south = (gx < NX - 1).astype(F32)
    west = (gy > 0).astype(F32)
    east = (gy < NY - 1).astype(F32)
    value = cin_ref[...].astype(F32)
    rim = value * sigmoid(value)
    rim = rim.astype(BF16).astype(F32)
    middle = jnp.concatenate([rim_ref[0:8] * north, rim, rim_ref[8:16] * south], axis=0)
    middle = middle.reshape(18, 8, CW)
    left = jnp.concatenate(
        [rim_ref[48:49] * north, rim_ref[16:32], rim_ref[64:65] * south], axis=0
    ) * west
    right = jnp.concatenate(
        [rim_ref[56:57] * north, rim_ref[32:48], rim_ref[72:73] * south], axis=0
    ) * east
    wide[0] = jnp.concatenate([left[:, None, :], middle[:, :7]], axis=1)
    wide[1] = middle
    wide[2] = jnp.concatenate([middle[:, 1:], right[:, None, :]], axis=1)
    total = value
    for p in range(3):
        for q in range(3):
            tap = wide[q, p : p + 16].reshape(128, CW)
            number = 3 * p + q
            total = total + mm(tap.astype(BF16), ck_ref[number])
            tapt_ref[number * CW : number * CW + CW] = tap.T.astype(BF16)
    base_ref[...] = total
    gouts = (cot_ref[...].astype(F32) * (1.0 / 128.0)).astype(BF16)
    gouts_ref[...] = gouts
    thr_ref[...] = mm(gouts, ow_ref[...], NT)


def step_kernel(
    src_ref, idx_ref, x_ref, ck_any, ow_any, cot_any, sel_ref, selt_ref, spread_ref, cin_ref, cw_ref,
    tw_ref, basis_ref, slot_ref, cell_ref, uw_ref,
    fa_ref, out_ref, f_ref,
    rows_ref, base_ref, thr_ref, gouts_ref, tapt_ref, rim_ref, ck_ref, ow_ref, cot_ref, wide, merged, folded, extra,
    own, planes, out_buf, rim_buf, shifted, slope, active_buf, near, spread, weight, pool, rows_buf, rows_mid,
    payload, half, mate, got0, got1, got2, sum1, sum2, gp2, slot_buf, slot_mid, slot_got,
    late, late_got, late_sum, late_all,
    xsem, wsem, fsem, ssem, rsem, ysend, yrecv, xsend, xrecv,
    csem, psem, asem, bsem, xback, yback, lsem, lxsem, lysem,
):
    gx, gy = lax.axis_index("gx"), lax.axis_index("gy")
    me = gx * NY + gy
    loads = []
    for part in range(4):
        bricks = pl.ds(16 * part, 16)
        loads.append(
            pltpu.make_async_copy(x_ref.at[bricks], shifted.at[bricks, pl.ds(0, CH)], xsem.at[part])
        )
        loads[-1].start()
    coarse_loads = [
        pltpu.make_async_copy(a, b, wsem.at[number])
        for number, (a, b) in enumerate(((ck_any, ck_ref), (ow_any, ow_ref), (cot_any, cot_ref)))
    ]
    for copy in coarse_loads:
        copy.start()
    face_to = []
    for bucket in range(NBUCKET):
        other = lax.rem(me + bucket_offset(bucket) + NDEV, NDEV)
        face_to.append((other // NY, lax.rem(other, NY)))
    rim_to = [
        (lax.rem(gx + dx + NX, NX), lax.rem(gy + dy + NY, NY)) for _, _, dx, dy in RIM_BLOCKS
    ]

    peers_x, peers_y = peers_of(gx, gy)
    partners = face_to + rim_to + [other for _, other in peers_x + peers_y]
    barrier = greet(partners)

    rim = cin_ref[...].astype(F32)
    rim = (rim * sigmoid(rim)).astype(BF16).astype(F32)
    cube = rim.reshape(16, 8, CW)
    rim_buf[0:8] = cube[15]
    rim_buf[8:16] = cube[0]
    rim_buf[16:32] = cube[:, 7, :]
    rim_buf[32:48] = cube[:, 0, :]
    rim_buf[48:56] = jnp.broadcast_to(cube[15, 7:8], (8, CW))
    rim_buf[56:64] = jnp.broadcast_to(cube[15, 0:1], (8, CW))
    rim_buf[64:72] = jnp.broadcast_to(cube[0, 7:8], (8, CW))
    rim_buf[72:80] = jnp.broadcast_to(cube[0, 0:1], (8, CW))

    low = lax.broadcasted_iota(jnp.int32, (32, 128), 1) < 64

    def flip(values):
        return jnp.concatenate([values[:, 64:], values[:, :64]], axis=1)

    def pack(values, upper):
        top, bottom = values[:32], values[32:]
        if upper:
            return jnp.where(low, flip(top), bottom)
        return jnp.where(low, top, flip(bottom))

    def extract(group, carry):
        rows = shifted[pl.ds(group * 4, 4), 0:CH].reshape(4 * CH, VOX)
        picked = mm(rows, sel_ref[...]).astype(BF16)
        for b in range(4):
            n = group * 4 + b
            brick = rows[64 * b : 64 * b + 64]
            both = picked[64 * b : 64 * b + 64]
            for face, plane in enumerate(
                (
                    pack(brick[:, 384:], True),
                    pack(brick[:, :128], False),
                    pack(both[:, :128], False),
                    pack(both[:, :128], True),
                    pack(both[:, 128:], False),
                    pack(both[:, 128:], True),
                )
            ):
                own[face * BD + n] = plane
                planes[face * BD + n] = plane
        return carry

    for part in range(4):
        loads[part].wait()
        lax.fori_loop(4 * part, 4 * part + 4, extract, 0)
    planes[528:544] = jnp.zeros((16, 32, 128), BF16)

    pl.semaphore_wait(barrier, len(partners))
    rim_copies = []
    for number, (first, rows, _, _) in enumerate(RIM_BLOCKS):
        rim_copies.append(
            pltpu.make_async_remote_copy(
                src_ref=rim_buf.at[pl.ds(first, rows)],
                dst_ref=rim_ref.at[pl.ds(first, rows)],
                send_sem=ssem.at[NBUCKET + number],
                recv_sem=rsem.at[NBUCKET + number],
                device_id=rim_to[number],
                device_id_type=MESH,
            )
        )
        rim_copies[-1].start()
    copies = []
    for face in range(6):

        def gather(slot, carry):
            out_buf[face * 2 * MFACE + slot] = own[face * BD + src_ref[slot, face]]
            return carry

        lax.fori_loop(0, 2 * MFACE, gather, 0)
        for bucket in (2 * face, 2 * face + 1):
            copies.append(
                pltpu.make_async_remote_copy(
                    src_ref=out_buf.at[pl.ds(bucket * MFACE, MFACE)],
                    dst_ref=planes.at[pl.ds(6 * BD + bucket * MFACE, MFACE)],
                    send_sem=ssem.at[bucket],
                    recv_sem=rsem.at[bucket],
                    device_id=face_to[bucket],
                    device_id_type=MESH,
                )
            )
            copies[-1].start()
    weight[...] = jnp.concatenate([cw_ref[k] for k in range(7)], axis=1)
    pool[...] = jnp.zeros_like(pool)
    embed = jnp.sum(tw_ref[...] * basis_ref[...], axis=1, keepdims=True)
    lane = lax.broadcasted_iota(jnp.int32, (CH, VOX), 1)
    by, bz = lane // 8 % 8, lane % 8
    keep = (by < 7, by > 0, bz < 7, bz > 0)
    tall_low = lax.broadcasted_iota(jnp.int32, (CH, 128), 1) < 64
    zero = jnp.zeros((CH, 128), BF16)

    def turned(values, shift):
        return jnp.concatenate([values[:, shift:], values[:, :shift]], axis=1)

    def shift_brick(n):
        field = shifted[n, 0:CH]
        flipped = turned(field, 64)
        shifted[n, 64:128, : VOX - 128] = flipped[:, : VOX - 128]
        shifted[n, 64:128, VOX - 128 :] = jnp.where(tall_low, flipped[:, VOX - 128 :], zero)
        back = turned(field, VOX - 64)
        shifted[n, 128:192, 128:] = back[:, 128:]
        shifted[n, 128:192, :128] = jnp.where(tall_low, zero, back[:, :128])
        for number, shift in enumerate((8, VOX - 8, 1, VOX - 1)):
            first = 192 + 64 * number
            moved = turned(field, shift)
            shifted[n, first : first + 64] = jnp.where(keep[number], moved, jnp.zeros_like(moved))
        shifted[n, 448:TROWS] = jnp.ones((16, VOX), BF16)
        hidden = mm(weight[...], shifted[n, 0:448]) + embed
        high = hidden.astype(BF16)
        active_buf[n] = high
        slope[n] = (hidden - high.astype(F32)).astype(BF16)

    def shift_two(pair, carry):
        shift_brick(2 * pair)
        shift_brick(2 * pair + 1)
        return carry

    lax.fori_loop(0, BD // 2, shift_two, 0)
    pool_lane = lax.broadcasted_iota(jnp.int32, (CH, 128), 1)

    for copy in coarse_loads:
        copy.wait()
    for copy in rim_copies:
        copy.wait_recv()
    rim_pass(gx, gy, cin_ref, rim_ref, ck_ref, ow_ref, cot_ref, base_ref, thr_ref, gouts_ref, tapt_ref, wide)
    for copy in copies:
        copy.wait_recv()

    def fine_step(step, carry):
        for pair in range(STEP // 2):
            n = step * STEP + 2 * pair
            lanes = slice(128 * pair, 128 * pair + 128)
            for face in range(6):
                one, two = planes[idx_ref[face, n]], planes[idx_ref[face, n + 1]]
                merged[face, 0:32, lanes] = jnp.where(low, one, flip(two))
                merged[face, 32:64, lanes] = jnp.where(low, flip(one), two)
        terms = [mm(cw_ref[1 + face], merged[face]) for face in range(6)]
        narrow = [terms[face].astype(BF16) for face in range(2, 6)]
        for pair in range(STEP // 2):
            lanes = slice(128 * pair, 128 * pair + 128)
            for half in range(2):
                one, two = narrow[2 * half][:, lanes], narrow[2 * half + 1][:, lanes]
                out = slice(128 * half, 128 * half + 128)
                folded[128 * pair : 128 * pair + 64, out] = jnp.where(tall_low, one, flip(two))
                folded[128 * pair + 64 : 128 * pair + 128, out] = jnp.where(tall_low, flip(one), two)
        extra[...] = mm(folded[...], selt_ref[...])
        for b in range(STEP):
            n = step * STEP + b
            lanes = slice(128 * (b // 2), 128 * (b // 2) + 128)
            plus, minus = terms[0][:, lanes], terms[1][:, lanes]
            plus = jnp.where(tall_low, 0.0, flip(plus) if b % 2 == 0 else plus)
            minus = jnp.where(tall_low, flip(minus) if b % 2 == 1 else minus, 0.0)
            total = jnp.zeros((CH, 128), F32)
            for j in range(4):
                part = slice(128 * j, 128 * j + 128)
                hidden = active_buf[n, :, part].astype(F32) + slope[n, :, part].astype(F32)
                hidden = hidden + extra[64 * b : 64 * b + 64, part]
                if j == 0:
                    hidden = hidden + minus
                if j == 3:
                    hidden = hidden + plus
                sigma = sigmoid(hidden)
                active = hidden * sigma
                active_buf[n, :, part] = active.astype(BF16)
                slope[n, :, part] = (sigma + active * (1.0 - sigma)).astype(BF16)
                total = total + active
            mean = jnp.sum(total, axis=1, keepdims=True) * (1.0 / VOX)
            pool[0:64] += jnp.where(pool_lane == n, mean, 0.0)
        return carry

    lax.fori_loop(0, BD // STEP, fine_step, 0)
    stored = pltpu.make_async_copy(active_buf, fa_ref, fsem)
    stored.start()

    pool[64:72] = jnp.broadcast_to(cell_ref[...], (8, 128))
    values = pool[...].astype(BF16)
    hot = (lax.broadcasted_iota(jnp.int32, (2 * NDEV, 128), 0) == slot_ref[...]).astype(BF16)
    rows_buf[...] = mm(hot, values, NT)[:, None, :].reshape(NY, 2 * NX, 1, 128)
    along_y = send_each(peers_y, lambda i: rows_buf.at[i], rows_mid.at[gy], ysend, yrecv)
    rows_mid[gy] = rows_buf[gy]

    def tap_lanes(k):
        return slice(128 * (k // 2), 128 * (k // 2) + 128)

    def tap_step(step, carry):
        bricks = [step * 2 + b % 2 + 32 * (b // 2) for b in range(4)]
        for b in range(4):
            for face in range(6):
                near[face, 32 * b : 32 * b + 32] = planes[idx_ref[face, bricks[b]]]
        for face in range(4):
            spread[face] = mm(near[2 + face], spread_ref[face]).astype(BF16)
        sums = []
        for b in range(4):
            n = bricks[b]
            above, below = near[0, 32 * b : 32 * b + 32], near[1, 32 * b : 32 * b + 32]
            plus = jnp.concatenate([flip(above), above], axis=0)
            minus = jnp.concatenate([below, flip(below)], axis=0)
            shifted[n, 64:128, VOX - 128 :] += jnp.where(tall_low, zero, plus)
            shifted[n, 128:192, :128] += jnp.where(tall_low, minus, zero)
            for number in range(4):
                rows = spread[number, 32 * b : 32 * b + 32]
                first = 192 + 64 * number
                shifted[n, first : first + 32] += rows[:, :VOX]
                shifted[n, first + 32 : first + 64] += rows[:, VOX:]
            sums.append(mm(shifted[n], slope[n], NT))
        for b in range(2):
            pair = step * 2 + b
            both = jnp.concatenate([sums[b], sums[b + 2]], axis=1).astype(BF16)
            for k in range(7):
                active_buf[2 * pair + k % 2, :, tap_lanes(k)] = both[64 * k : 64 * k + 64]
            active_buf[2 * pair + 1, 0:16, tap_lanes(7)] = both[448:TROWS]
        return carry

    def taps(first, end):
        lax.fori_loop(first, end, tap_step, 0)

    stored.wait()
    taps(0, 3)
    for copy in along_y:
        copy.wait_recv()
    along_x = send_each(
        peers_x, lambda i: rows_mid.at[:, pl.ds(2 * i, 2)], rows_ref.at[gx], xsend, xrecv
    )
    rows_ref[gx] = rows_mid[:, pl.ds(2 * gx, 2)]
    taps(3, 6)
    for copy in along_x:
        copy.wait_recv()

    x, c = gx // 2, lax.rem(gx, 2)
    y, z = gy // 4, lax.rem(gy, 4)
    place = (x, y, z)

    def device(axis, index):
        where = list(place)
        where[axis] = index
        return (where[0] * 2 + c, where[1] * 4 + where[2])

    peers = [
        [lax.rem(place[axis] + step, 4) for step in (1, 2, 3)] for axis in range(3)
    ]
    other_core = (x * 2 + 1 - c, gy)
    rows = rows_ref[...].reshape(2 * NDEV, 1, 128).reshape(2 * NDEV, 128).astype(BF16)
    pick = (lax.broadcasted_iota(jnp.int32, (8, 128), 1) == 64).astype(BF16)
    cells = mm(pick, rows, NT)[0:1].astype(jnp.int32)
    hot = lax.broadcasted_iota(jnp.int32, (128, 2 * NDEV), 0) + 1 == cells
    hot = hot.astype(BF16)
    summed = mm(hot, rows)[:, 0:CH]
    high = summed.astype(BF16)
    rest = (summed - high.astype(F32)).astype(BF16)
    uw = uw_ref[...]
    pre = base_ref[...] + mm(high, uw) + mm(rest, uw)
    sigma = sigmoid(pre)
    active = pre * sigma
    act = active.astype(BF16)
    out_ref[...] = (pre + mm(act, ow_ref[...])).astype(BF16)
    gouts = gouts_ref[...]
    gpre = gouts.astype(F32) + thr_ref[...] * (sigma + active * (1.0 - sigma))
    gpre = gpre.astype(BF16)
    gp = mm(gpre, uw, NT)
    gp = jnp.concatenate([gp, gp], axis=1).astype(BF16)
    slot_buf[...] = mm(hot.astype(F32).T.astype(BF16), gp)[:, None, :].reshape(NX, 2 * NY, 1, 128)
    for number in range(9):
        part = mm(tapt_ref[number * CW : number * CW + CW], gpre).astype(BF16)
        payload[512 * number : 512 * number + 256] = part[:, :128]
        payload[512 * number + 256 : 512 * number + 512] = part[:, 128:]
    part = mm(active.T.astype(BF16), gouts).astype(BF16)
    payload[4608:4864] = part[:, :128]
    payload[4864:5120] = part[:, 128:]
    pooled = jnp.concatenate([summed, summed], axis=1).T[0:CH]
    pooled_high = pooled.astype(BF16)
    pooled_rest = (pooled - pooled_high.astype(F32)).astype(BF16)
    part = (mm(pooled_high, gpre) + mm(pooled_rest, gpre)).astype(BF16)
    payload[5120:5184] = part[:, :128]
    payload[5184:5248] = part[:, 128:]

    payload[GROWS:PAYLOAD] = jnp.zeros((PAYLOAD - GROWS, 128), BF16)

    def remote(src, dst, sems, index, target):
        copy = pltpu.make_async_remote_copy(
            src_ref=src,
            dst_ref=dst,
            send_sem=sems.at[(0,) + index],
            recv_sem=sems.at[(1,) + index],
            device_id=target,
            device_id_type=MESH,
        )
        copy.start()
        return copy

    def cross(g):
        return remote(
            payload.at[pl.ds(2048 * g + (1 - c) * 1024, 1024)],
            mate.at[pl.ds(1024 * g, 1024)],
            csem, (g,), other_core,
        )

    def tap_sums():
        hot_rows = (lax.broadcasted_iota(jnp.int32, (2 * NDEV, 128), 0) == slot_ref[...]).astype(F32)
        back_rows = slot_got[...].reshape(2 * NDEV, 1, 128).reshape(2 * NDEV, 128).astype(BF16)
        mine = mm(hot_rows.T.astype(BF16), back_rows)
        gp2[...] = jnp.where(low, mine[0:32], mine[32:64]) * (1.0 / VOX)
        for k in range(7):

            def add(pair, total):
                block = active_buf[2 * pair + k % 2, :, tap_lanes(k)].astype(F32)
                return total + block * gp2[pl.ds(pair, 1)]

            total = lax.fori_loop(0, 32, add, jnp.zeros((CH, 128), F32), unroll=4)
            late[64 * k : 64 * k + 64] = total.astype(BF16)

        def add_plain(pair, total):
            block = active_buf[2 * pair + 1, 0:16, tap_lanes(7)].astype(F32)
            return total + block * gp2[pl.ds(pair, 1)]

        total = lax.fori_loop(0, 32, add_plain, jnp.zeros((16, 128), F32), unroll=4)
        row = lax.broadcasted_iota(jnp.int32, (16, 128), 0)
        late[448:TROWS] = (total * (1.0 + row.astype(F32) / 16.0)).astype(BF16)
        late[TROWS:LATE] = jnp.zeros((LATE - TROWS, 128), BF16)

    got = (got0, got1, got2)
    size = (256, 64, 16)
    phase = [[None] * 3 for _ in range(3)]

    def launch(p, g, src, base):
        axis = (g + p) % 3
        out = []
        for s in range(3):
            index = peers[axis][s]
            out.append(
                remote(
                    src.at[pl.ds(base + index * size[p], size[p])],
                    got[p].at[pl.ds((3 * g + s) * size[p], size[p])],
                    psem, (p, g, s), device(axis, index),
                )
            )
        return out

    def gathered(p, g, src, base):
        axis = (g + p) % 3
        for copy in phase[p][g]:
            copy.wait_recv()
        total = src[pl.ds(base + place[axis] * size[p], size[p])].astype(F32)
        for s in range(3):
            first = (3 * g + s) * size[p]
            total = total + got[p][first : first + size[p]].astype(F32)
        return total.astype(BF16)

    def crossed(g):
        core[g].wait_recv()
        half[1024 * g : 1024 * g + 1024] = (
            payload[pl.ds(2048 * g + c * 1024, 1024)].astype(F32)
            + mate[1024 * g : 1024 * g + 1024].astype(F32)
        ).astype(BF16)
        phase[0][g] = launch(0, g, half, 1024 * g)

    def first_sum(g):
        sum1[256 * g : 256 * g + 256] = gathered(0, g, half, 1024 * g)
        phase[1][g] = launch(1, g, sum1, 256 * g)

    def second_sum(g):
        sum2[64 * g : 64 * g + 64] = gathered(1, g, sum1, 256 * g)
        phase[2][g] = launch(2, g, sum2, 64 * g)

    bases = []
    for g in range(3):
        i0, i1, i2 = place[g % 3], place[(g + 1) % 3], place[(g + 2) % 3]
        start = 2048 * g + c * 1024
        bases.append((start + i0 * 256, start + i0 * 256 + i1 * 64, start + i0 * 256 + i1 * 64 + i2 * 16))
    back = [[None] * 3 for _ in range(3)]

    def share(p, g):
        axis = (g + p) % 3
        where = f_ref.at[pl.ds(bases[g][p], size[p])]
        back[p][g] = [
            remote(where, where, asem, (p, g, s), device(axis, peers[axis][s])) for s in range(3)
        ]

    def third_sum(g):
        f_ref[pl.ds(bases[g][2], 16)] = gathered(2, g, sum2, 64 * g)
        share(2, g)

    def onward(p, g):
        for copy in back[p + 1][g]:
            copy.wait_recv()
        share(p, g)

    last = []

    def across(g):
        for copy in back[0][g]:
            copy.wait_recv()
        where = f_ref.at[pl.ds(2048 * g + c * 1024, 1024)]
        last.append(remote(where, where, bsem, (g,), other_core))

    back_x = send_each(peers_x, lambda i: slot_buf.at[i], slot_mid.at[gx], xback.at[0], xback.at[1])
    slot_mid[gx] = slot_buf[gx]
    core = [cross(g) for g in range(3)]
    taps(6, 8)
    for copy in back_x:
        copy.wait_recv()
    back_y = send_each(
        peers_y, lambda i: slot_mid.at[:, pl.ds(2 * i, 2)], slot_got.at[gy], yback.at[0], yback.at[1]
    )
    slot_got[gy] = slot_mid[:, pl.ds(2 * gy, 2)]
    for g in range(3):
        crossed(g)
    taps(8, 12)
    for g in range(3):
        first_sum(g)
    taps(12, 16)
    for g in range(3):
        second_sum(g)
    for copy in back_y:
        copy.wait_recv()
    tap_sums()
    late_y = send_each(
        peers_y, lambda i: late.at[pl.ds(32 * i, 32)], late_got.at[gy], lsem.at[0], lsem.at[1]
    )
    late_got[gy] = late[pl.ds(pl.multiple_of(32 * gy, 32), 32)]
    for g in range(3):
        third_sum(g)
    for copy in late_y:
        copy.wait_recv()
    total = late_got[0].astype(F32)
    for i in range(1, NY):
        total = total + late_got[i].astype(F32)
    late_sum[...] = total.astype(BF16)
    late_x = send_each(peers_x, lambda i: late_sum, late_all.at[gx], lxsem.at[0], lxsem.at[1])
    late_all[gx] = late_sum[...]
    for g in range(3):
        onward(1, g)
    for copy in late_x:
        copy.wait_recv()
    total = late_all[0].astype(F32)
    for i in range(1, NX):
        total = total + late_all[i].astype(F32)
    where = f_ref.at[pl.ds(pl.multiple_of(PAYLOAD + 32 * gy, 32), 32)]
    where[...] = total.astype(BF16)
    late_back = send_each(peers_y, lambda i: where, where, lysem.at[0], lysem.at[1])
    for g in range(3):
        onward(0, g)
    for g in range(3):
        across(g)
    for copy in last + late_back:
        copy.wait_recv()
    for copy in core + last + along_x + along_y + copies + rim_copies + back_x + back_y + late_y + late_x + late_back:
        copy.wait_send()
    for p in range(3):
        for g in range(3):
            for copy in phase[p][g] + back[p][g]:
                copy.wait_send()


def result_kernel(f_ref, basis_ref, fa_ref, co_ref, fa_out, co_out, conv_ref, time_ref, up_ref, kernel_ref, out_ref, sem):
    moved = []
    for part in range(8):
        bricks = pl.ds(8 * part, 8)
        moved.append(pltpu.make_async_copy(fa_ref.at[bricks], fa_out.at[bricks], sem.at[part]))
        moved[-1].start()
    co_out[...] = co_ref[...]
    for number in range(9):
        kernel_ref[number, :, :128] = f_ref[512 * number : 512 * number + 256].astype(F32)
        kernel_ref[number, :, 128:] = f_ref[512 * number + 256 : 512 * number + 512].astype(F32)
    out_ref[:, :128] = f_ref[4608:4864].astype(F32)
    out_ref[:, 128:] = f_ref[4864:5120].astype(F32)
    up_ref[:, :128] = f_ref[5120:5184].astype(F32)
    up_ref[:, 128:] = f_ref[5184:5248].astype(F32)
    tail = f_ref[PAYLOAD : PAYLOAD + TROWS].astype(F32)
    tail = tail + jnp.concatenate([tail[:, 64:], tail[:, :64]], axis=1)
    for k in range(7):
        block = tail[64 * k : 64 * k + 64]
        conv_ref[k] = jnp.concatenate([block, block], axis=0).T[:CH, :CH]
    row = lax.broadcasted_iota(jnp.int32, (16, 128), 0).astype(F32)
    plain = jnp.sum(tail[448:464] / (1.0 + row / 16.0), axis=0, keepdims=True) / 16.0
    column = jnp.broadcast_to(plain, (128, 128)).T[:CH, 0:1]
    time_ref[...] = column * basis_ref[...]
    for copy in moved:
        copy.wait()


def time_features(timestep, channels):
    half_count = channels // 2
    frequency = jnp.exp(-math.log(10000.0) * jnp.arange(half_count, dtype=jnp.float32) / half_count)
    angles = timestep[0].astype(jnp.float32) * frequency
    return jnp.concatenate([jnp.sin(angles), jnp.cos(angles)])


def shards(
    fine_in, neighbours, parent_dev, parent_cell, timestep, conv_weight, time_weight, up_weight,
    coarse_in, coarse_kernel_in, out_weight, coarse_cot,
):
    sds = jax.ShapeDtypeStruct
    anywhere = pl.BlockSpec(memory_space=pl.ANY)
    selector = face_selector()
    basis = time_features(timestep, CH)[None, :]
    cin = coarse_in.reshape(128, CW)
    cot = coarse_cot.reshape(128, CW)

    index, source, slot, cell_lane = pl.pallas_call(
        route_kernel,
        out_shape=(
            sds((6, BD), jnp.int32), sds((2 * MFACE, 6), jnp.int32), sds((1, 128), jnp.int32),
            sds((1, 128), F32),
        ),
        in_specs=[VMEM] * 3,
        out_specs=(VMEM,) * 4,
        name="routes",
    )(neighbours.T, parent_dev.T, parent_cell[None, :])

    fine_act, coarse_out, summed = pl.pallas_call(
        step_kernel,
        out_shape=(
            sds((BD, CH, VOX), BF16), sds((128, CW), BF16), sds((PAYLOAD + LATE, 128), BF16),
        ),
        in_specs=[SMEM, SMEM] + [anywhere] * 4 + [VMEM] * 10,
        out_specs=(anywhere, VMEM, VMEM),
        scratch_shapes=[
            pltpu.VMEM((NX, NY, 2, 1, 128), F32),
            pltpu.VMEM((128, CW), F32),
            pltpu.VMEM((128, CW), F32),
            pltpu.VMEM((128, CW), BF16),
            pltpu.VMEM((9 * CW, 128), BF16),
            pltpu.VMEM((80, CW), F32),
            pltpu.VMEM((9, CW, CW), BF16),
            pltpu.VMEM((CW, CW), BF16),
            pltpu.VMEM((128, CW), BF16),
            pltpu.VMEM((3, 18, 8, CW), F32),
            pltpu.VMEM((6, CH, 64 * STEP), BF16),
            pltpu.VMEM((64 * STEP, 256), BF16),
            pltpu.VMEM((64 * STEP, VOX), F32),
            pltpu.VMEM((6 * BD, 32, 128), BF16),
            pltpu.VMEM((544, 32, 128), BF16),
            pltpu.VMEM((NBUCKET * MFACE, 32, 128), BF16),
            pltpu.VMEM((80, CW), F32),
            pltpu.VMEM((BD, TROWS, VOX), BF16),
            pltpu.VMEM((BD, CH, VOX), BF16),
            pltpu.VMEM((BD, CH, VOX), BF16),
            pltpu.VMEM((6, 128, 128), BF16),
            pltpu.VMEM((4, 128, 2 * VOX), BF16),
            pltpu.VMEM((CH, 448), BF16),
            pltpu.VMEM((128, 128), F32),
            pltpu.VMEM((NY, 2 * NX, 1, 128), F32),
            pltpu.VMEM((NY, 2 * NX, 1, 128), F32),
            pltpu.VMEM((PAYLOAD, 128), BF16),
            pltpu.VMEM((3 * 1024, 128), BF16),
            pltpu.VMEM((3 * 1024, 128), BF16),
            pltpu.VMEM((9 * 256, 128), BF16),
            pltpu.VMEM((9 * 64, 128), BF16),
            pltpu.VMEM((9 * 16, 128), BF16),
            pltpu.VMEM((3 * 256, 128), BF16),
            pltpu.VMEM((3 * 64, 128), BF16),
            pltpu.VMEM((32, 128), F32),
            pltpu.VMEM((NX, 2 * NY, 1, 128), F32),
            pltpu.VMEM((NX, 2 * NY, 1, 128), F32),
            pltpu.VMEM((NY, NX, 2, 1, 128), F32),
            pltpu.VMEM((LATE, 128), BF16),
            pltpu.VMEM((NY, 32, 128), BF16),
            pltpu.VMEM((32, 128), BF16),
            pltpu.VMEM((NX, 32, 128), BF16),
            pltpu.SemaphoreType.DMA((4,)),
            pltpu.SemaphoreType.DMA((3,)),
            pltpu.SemaphoreType.DMA,
            pltpu.SemaphoreType.DMA((20,)),
            pltpu.SemaphoreType.DMA((20,)),
            pltpu.SemaphoreType.DMA((NY - 1,)),
            pltpu.SemaphoreType.DMA((NY - 1,)),
            pltpu.SemaphoreType.DMA((NX - 1,)),
            pltpu.SemaphoreType.DMA((NX - 1,)),
            pltpu.SemaphoreType.DMA((2, 3)),
            pltpu.SemaphoreType.DMA((2, 3, 3, 3)),
            pltpu.SemaphoreType.DMA((2, 3, 3, 3)),
            pltpu.SemaphoreType.DMA((2, 3)),
            pltpu.SemaphoreType.DMA((2, NX - 1)),
            pltpu.SemaphoreType.DMA((2, NY - 1)),
            pltpu.SemaphoreType.DMA((2, NY - 1)),
            pltpu.SemaphoreType.DMA((2, NX - 1)),
            pltpu.SemaphoreType.DMA((2, NY - 1)),
        ],
        compiler_params=pltpu.CompilerParams(
            collective_id=0, has_side_effects=True, vmem_limit_bytes=62 * 2**20
        ),
        name="step",
    )(
        source, index, fine_in, coarse_kernel_in, out_weight, cot, jnp.asarray(selector, BF16),
        jnp.asarray(selector.T, BF16), jnp.asarray(face_spreader(selector), BF16), cin, conv_weight,
        time_weight, basis, slot, cell_lane, up_weight,
    )

    outs = pl.pallas_call(
        result_kernel,
        out_shape=(
            sds((BD, CH, VOX), BF16), sds((128, CW), BF16),
            sds((7, CH, CH), F32), sds((CH, CH), F32), sds((CH, CW), F32), sds((9, CW, CW), F32),
            sds((CW, CW), F32),
        ),
        in_specs=[VMEM, VMEM, anywhere, VMEM],
        out_specs=(anywhere,) + (VMEM,) * 6,
        scratch_shapes=[pltpu.SemaphoreType.DMA((8,))],
        compiler_params=pltpu.CompilerParams(vmem_limit_bytes=32 * 2**20),
        name="results",
    )(summed, basis, fine_act, coarse_out)
    return (outs[0], outs[1].reshape(16, 8, CW)) + tuple(outs[2:])


def solution(mesh):
    both = ("gx", "gy")
    return jax.shard_map(
        shards,
        mesh=mesh,
        in_specs=(
            P(both, None, None), P(both, None), P(both, None), P(both), P(), P(), P(), P(),
            P("gx", "gy", None), P(), P(), P("gx", "gy", None),
        ),
        out_specs=(P(both, None, None), P("gx", "gy", None), P(), P(), P(), P(), P()),
        check_vma=False,
    )
```

time: 113 us -> 104 us (0.920)
  Pallas kernels: 109 us -> 97.7 us
  local copies, waits for them, and re-layouts: 1.96 us -> 4.48 us
    pallas_call x3 -> x1, Pallas kernels: 103 us -> 92.2 us  [shards(): pl.pallas_call(step_kernel, out_shape=(sds((BD, CH, VOX), BF16), sds((128...]
    unnamed x20 -> x8, local copies, waits for them, and re-layouts: 1.96 us -> 4.48 us
where the time goes in v3:
time: 104 us
  Pallas kernels  97.7 us (94%)
  local copies, waits for them, and re-layouts  4.48 us (4%)
  between operations  1.31 us (1%)
    pallas_call x1, Pallas kernels, shards(): pl.pallas_call(step_kernel, out_shape=(sds((BD, CH, VOX), BF16), sds((128...  92.2 us
    unnamed x8, local copies, waits for them, and re-layouts  4.48 us
    pallas_call x1, Pallas kernels, shards(): pl.pallas_call(result_kernel, out_shape=(sds((BD, CH, VOX), BF16), sds((1...  3.68 us

profile of v3, /device:TPU:1, one launch (start us, length us, event | category | flops | bytes accessed | tf_op | source)
XLA Modules:
  0.0 104.2 jit_solution(5388072386446175552)
XLA Ops:
  1.3 0.6 maximum_bitcast_fusion.basis_ref
  1.9 0.0 copy-start.3
  1.9 1.9 %routes.1 = (s32[6,64]{1,0:T(8,128)}, s32[24,6]{1,0:T(8,128)}, s32[1,128]{1,0:T(1,128)}, f32[1,128]{1,0:T(1,128)}) custom-call(s32[6,64]{1,0:T(8,128)} %bitcast.11, s32[1,64]{1,0:T(1,128)} %bitcast.12, s32[1,64]{1,0:T(1,128)} %bitcast.13), custom_call_target="tpu_custom_call" | custom-call | tf_op jit(solution)/shard_map/routes/pallas_call | solution.py:718
  3.8 92.2 %step.1 = (bf16[64,64,512]{2,1,0:T(8,128)(2,1)}, bf16[128,256]{1,0:T(8,128)(2,1)}, bf16[6656,128]{1,0:T(8,128)(2,1)}) custom-call(s32[24,6]{1,0:T(8,128)} %get-tuple-element.21.src_ref, s32[6,64]{1,0:T(8,128)} %get-tuple-element.22.idx_ref, bf16[64,64,512]{2,1,0:T(8,128)(2,1)} %x_ref.1, bf16[9,256,256]{2,1,0:T(8,128)(2,1)} %ck_any.1, ...), custom_call_target="tpu_custom_call" | custom-call | tf_op jit(solution)/shard_map/step/pallas_call | solution.py:729
  96.0 0.0 copy-done.3
  96.0 0.0 copy-start
  96.0 2.2 %copy-done = bf16[64,64,512]{2,1,0:T(8,128)(2,1)S(1)} copy-done((bf16[64,64,512]{2,1,0:T(8,128)(2,1)S(1)}, bf16[64,64,512]{2,1,0:T(8,128)(2,1)}, u32[]{:S(2)}) %copy-start) | copy-done | bytes 4194328
  98.2 0.0 copy-start.1
  98.2 1.5 %copy-done.1 = bf16[6656,128]{1,0:T(8,128)(2,1)S(1)} copy-done((bf16[6656,128]{1,0:T(8,128)(2,1)S(1)}, bf16[6656,128]{1,0:T(8,128)(2,1)}, u32[]{:S(2)}) %copy-start.1) | copy-done | bytes 1703960
  99.6 0.0 copy-start.2
  99.6 0.8 copy-done.2
  100.5 3.7 %results.1 = (bf16[64,64,512]{2,1,0:T(8,128)(2,1)}, bf16[128,256]{1,0:T(8,128)(2,1)}, f32[7,64,64]{2,1,0:T(8,128)}, f32[64,64]{1,0:T(8,128)}, f32[64,256]{1,0:T(...) custom-call(bf16[6656,128]{1,0:T(8,128)(2,1)S(1)} %copy-done.1, f32[1,64]{1,0:T(1,128)S(1)} %copy-done.3, ...), custom_call_target="tpu_custom_call" | custom-call | tf_op jit(solution)/shard_map/results/pallas_call | solution.py:808
  (1 shorter events, 0.0 us)
Async XLA Ops:
  1.9 94.1 %copy-start.3 = (f32[1,64]{1,0:T(1,128)S(1)}, f32[1,64]{1,0:T(1,128)}, u32[]{:S(2)}) copy-start(f32[1,64]{1,0:T(1,128)} %maximum_bitcast_fusion.basis_ref) | copy-start | bytes 772
  96.0 2.2 %copy-start = (bf16[64,64,512]{2,1,0:T(8,128)(2,1)S(1)}, bf16[64,64,512]{2,1,0:T(8,128)(2,1)}, u32[]{:S(2)}) copy-start(bf16[64,64,512]{2,1,0:T(8,128)(2,1)} %get-tuple-element.26.fa_ref) | copy-start | bytes 12582916
  98.2 1.5 %copy-start.1 = (bf16[6656,128]{1,0:T(8,128)(2,1)S(1)}, bf16[6656,128]{1,0:T(8,128)(2,1)}, u32[]{:S(2)}) copy-start(bf16[6656,128]{1,0:T(8,128)(2,1)} %get-tuple-element.25.f_ref) | copy-start | bytes 5111812
  99.6 0.8 copy-start.2

commit v4 on v3

--- a/solution.py
+++ b/solution.py
@@ -239,33 +239,64 @@
             return jnp.where(low, flip(top), bottom)
         return jnp.where(low, top, flip(bottom))
 
-    def extract(group, carry):
-        rows = shifted[pl.ds(group * 4, 4), 0:CH].reshape(4 * CH, VOX)
-        picked = mm(rows, sel_ref[...]).astype(BF16)
+    def keep_plane(row, plane):
+        own[row] = plane
+        planes[row] = plane
+
+    def extract_x(group, carry):
         for b in range(4):
             n = group * 4 + b
-            brick = rows[64 * b : 64 * b + 64]
-            both = picked[64 * b : 64 * b + 64]
-            for face, plane in enumerate(
-                (
-                    pack(brick[:, 384:], True),
-                    pack(brick[:, :128], False),
-                    pack(both[:, :128], False),
-                    pack(both[:, :128], True),
-                    pack(both[:, 128:], False),
-                    pack(both[:, 128:], True),
+            keep_plane(n, pack(shifted[n, 0:CH, VOX - 128 :], True))
+            keep_plane(BD + n, pack(shifted[n, 0:CH, :128], False))
+        return carry
+
+    def extract_yz(first):
+        def body(group, carry):
+            rows = shifted[pl.ds(group * 4, 4), 0:CH].reshape(4 * CH, VOX)
+            lanes = slice(64 * (first - 2), 64 * (first - 2) + 128)
+            picked = mm(rows, sel_ref[:, lanes]).astype(BF16)
+            for b in range(4):
+                n = group * 4 + b
+                both = picked[64 * b : 64 * b + 64]
+                keep_plane(first * BD + n, pack(both, False))
+                keep_plane((first + 1) * BD + n, pack(both, True))
+            return carry
+
+        return body
+
+    copies = []
+
+    def send_faces(first):
+        for face in (first, first + 1):
+
+            def gather(slot, carry):
+                out_buf[face * 2 * MFACE + slot] = own[face * BD + src_ref[slot, face]]
+                return carry
+
+            lax.fori_loop(0, 2 * MFACE, gather, 0, unroll=4)
+            for bucket in (2 * face, 2 * face + 1):
+                copies.append(
+                    pltpu.make_async_remote_copy(
+                        src_ref=out_buf.at[pl.ds(bucket * MFACE, MFACE)],
+                        dst_ref=planes.at[pl.ds(6 * BD + bucket * MFACE, MFACE)],
+                        send_sem=ssem.at[bucket],
+                        recv_sem=rsem.at[bucket],
+                        device_id=face_to[bucket],
+                        device_id_type=MESH,
+                    )
                 )
-            ):
-                own[face * BD + n] = plane
-                planes[face * BD + n] = plane
-        return carry
+                copies[-1].start()
 
     for part in range(4):
         loads[part].wait()
-        lax.fori_loop(4 * part, 4 * part + 4, extract, 0)
+        lax.fori_loop(4 * part, 4 * part + 4, extract_x, 0)
     planes[528:544] = jnp.zeros((16, 32, 128), BF16)
-
     pl.semaphore_wait(barrier, len(partners))
+    send_faces(0)
+    lax.fori_loop(0, 16, extract_yz(4), 0)
+    send_faces(4)
+    lax.fori_loop(0, 16, extract_yz(2), 0)
+    send_faces(2)
     rim_copies = []
     for number, (first, rows, _, _) in enumerate(RIM_BLOCKS):
         rim_copies.append(
@@ -279,26 +310,7 @@
             )
         )
         rim_copies[-1].start()
-    copies = []
-    for face in range(6):
-
-        def gather(slot, carry):
-            out_buf[face * 2 * MFACE + slot] = own[face * BD + src_ref[slot, face]]
-            return carry
-
-        lax.fori_loop(0, 2 * MFACE, gather, 0)
-        for bucket in (2 * face, 2 * face + 1):
-            copies.append(
-                pltpu.make_async_remote_copy(
-                    src_ref=out_buf.at[pl.ds(bucket * MFACE, MFACE)],
-                    dst_ref=planes.at[pl.ds(6 * BD + bucket * MFACE, MFACE)],
-                    send_sem=ssem.at[bucket],
-                    recv_sem=rsem.at[bucket],
-                    device_id=face_to[bucket],
-                    device_id_type=MESH,
-                )
-            )
-            copies[-1].start()
+
     weight[...] = jnp.concatenate([cw_ref[k] for k in range(7)], axis=1)
     pool[...] = jnp.zeros_like(pool)
     embed = jnp.sum(tw_ref[...] * basis_ref[...], axis=1, keepdims=True)
@@ -507,11 +519,17 @@
         return copy
 
     def cross(g):
-        return remote(
-            payload.at[pl.ds(2048 * g + (1 - c) * 1024, 1024)],
-            mate.at[pl.ds(1024 * g, 1024)],
-            csem, (g,), other_core,
-        )
+        out = []
+        for s in range(4):
+            index = peers[g][s] if s < 3 else place[g]
+            out.append(
+                remote(
+                    payload.at[pl.ds(2048 * g + (1 - c) * 1024 + index * 256, 256)],
+                    mate.at[pl.ds(1024 * g + index * 256, 256)],
+                    csem, (g, s), other_core,
+                )
+            )
+        return out
 
     def tap_sums():
         hot_rows = (lax.broadcasted_iota(jnp.int32, (2 * NDEV, 128), 0) == slot_ref[...]).astype(F32)
@@ -565,12 +583,20 @@
         return total.astype(BF16)
 
     def crossed(g):
-        core[g].wait_recv()
-        half[1024 * g : 1024 * g + 1024] = (
-            payload[pl.ds(2048 * g + c * 1024, 1024)].astype(F32)
-            + mate[1024 * g : 1024 * g + 1024].astype(F32)
-        ).astype(BF16)
-        phase[0][g] = launch(0, g, half, 1024 * g)
+        phase[0][g] = []
+        for s in range(4):
+            index = peers[g][s] if s < 3 else place[g]
+            core[g][s].wait_recv()
+            mine = pl.ds(pl.multiple_of(1024 * g + index * 256, 256), 256)
+            theirs = pl.ds(pl.multiple_of(2048 * g + c * 1024 + index * 256, 256), 256)
+            half[mine] = (payload[theirs].astype(F32) + mate[mine].astype(F32)).astype(BF16)
+            if s < 3:
+                phase[0][g].append(
+                    remote(
+                        half.at[mine], got0.at[pl.ds((3 * g + s) * 256, 256)], psem, (0, g, s),
+                        device(g, index),
+                    )
+                )
 
     def first_sum(g):
         sum1[256 * g : 256 * g + 256] = gathered(0, g, half, 1024 * g)
@@ -605,11 +631,13 @@
 
     last = []
 
-    def across(g):
-        for copy in back[0][g]:
-            copy.wait_recv()
-        where = f_ref.at[pl.ds(2048 * g + c * 1024, 1024)]
-        last.append(remote(where, where, bsem, (g,), other_core))
+    def hand_over(g, s, index):
+        where = f_ref.at[pl.ds(2048 * g + c * 1024 + index * 256, 256)]
+        last.append(remote(where, where, bsem, (g, s), other_core))
+
+    def across(g, s):
+        back[0][g][s].wait_recv()
+        hand_over(g, s, lax.rem(place[g] + 3 - s, 4))
 
     back_x = send_each(peers_x, lambda i: slot_buf.at[i], slot_mid.at[gx], xback.at[0], xback.at[1])
     slot_mid[gx] = slot_buf[gx]
@@ -658,11 +686,13 @@
     late_back = send_each(peers_y, lambda i: where, where, lysem.at[0], lysem.at[1])
     for g in range(3):
         onward(0, g)
-    for g in range(3):
-        across(g)
+        hand_over(g, 3, place[g])
+    for s in range(3):
+        for g in range(3):
+            across(g, s)
     for copy in last + late_back:
         copy.wait_recv()
-    for copy in core + last + along_x + along_y + copies + rim_copies + back_x + back_y + late_y + late_x + late_back:
+    for copy in core[0] + core[1] + core[2] + last + along_x + along_y + copies + rim_copies + back_x + back_y + late_y + late_x + late_back:
         copy.wait_send()
     for p in range(3):
         for g in range(3):
@@ -670,18 +700,42 @@
                 copy.wait_send()
 
 
-def result_kernel(f_ref, basis_ref, fa_ref, co_ref, fa_out, co_out, conv_ref, time_ref, up_ref, kernel_ref, out_ref, sem):
-    moved = []
+def result_kernel(
+    f_any, basis_ref, fa_ref, co_ref, fa_out, co_out, conv_ref, time_ref, up_ref, kernel_any, out_any,
+    f_ref, wide, fa_buf, co_buf, sem, fsem, ksem,
+):
+    loads = {}
+    for part in list(range(11)) + [12]:
+        rows = pl.ds(512 * part, 512)
+        loads[part] = pltpu.make_async_copy(f_any.at[rows], f_ref.at[rows], fsem.at[part])
+        loads[part].start()
+    held = [(co_ref, co_buf, co_out)]
     for part in range(8):
         bricks = pl.ds(8 * part, 8)
-        moved.append(pltpu.make_async_copy(fa_ref.at[bricks], fa_out.at[bricks], sem.at[part]))
+        held.append((fa_ref.at[bricks], fa_buf.at[bricks], fa_out.at[bricks]))
+    fetched = [
+        pltpu.make_async_copy(src, buf, sem.at[0, part]) for part, (src, buf, _) in enumerate(held)
+    ]
+    for copy in fetched:
+        copy.start()
+    moved = []
+
+    def pass_on(part):
+        fetched[part].wait()
+        moved.append(pltpu.make_async_copy(held[part][1], held[part][2], sem.at[1, part]))
         moved[-1].start()
-    co_out[...] = co_ref[...]
-    for number in range(9):
-        kernel_ref[number, :, :128] = f_ref[512 * number : 512 * number + 256].astype(F32)
-        kernel_ref[number, :, 128:] = f_ref[512 * number + 256 : 512 * number + 512].astype(F32)
-    out_ref[:, :128] = f_ref[4608:4864].astype(F32)
-    out_ref[:, 128:] = f_ref[4864:5120].astype(F32)
+
+    for number in range(10):
+        loads[number].wait()
+        wide[number, :, :128] = f_ref[512 * number : 512 * number + 256].astype(F32)
+        wide[number, :, 128:] = f_ref[512 * number + 256 : 512 * number + 512].astype(F32)
+        target = kernel_any.at[number] if number < 9 else out_any
+        moved.append(pltpu.make_async_copy(wide.at[number], target, ksem.at[number]))
+        moved[-1].start()
+        if number < 9:
+            pass_on(number)
+    loads[10].wait()
+    loads[12].wait()
     up_ref[:, :128] = f_ref[5120:5184].astype(F32)
     up_ref[:, 128:] = f_ref[5184:5248].astype(F32)
     tail = f_ref[PAYLOAD : PAYLOAD + TROWS].astype(F32)
@@ -785,10 +839,10 @@
             pltpu.SemaphoreType.DMA((NY - 1,)),
             pltpu.SemaphoreType.DMA((NX - 1,)),
             pltpu.SemaphoreType.DMA((NX - 1,)),
-            pltpu.SemaphoreType.DMA((2, 3)),
+            pltpu.SemaphoreType.DMA((2, 3, 4)),
             pltpu.SemaphoreType.DMA((2, 3, 3, 3)),
             pltpu.SemaphoreType.DMA((2, 3, 3, 3)),
-            pltpu.SemaphoreType.DMA((2, 3)),
+            pltpu.SemaphoreType.DMA((2, 3, 4)),
             pltpu.SemaphoreType.DMA((2, NX - 1)),
             pltpu.SemaphoreType.DMA((2, NY - 1)),
             pltpu.SemaphoreType.DMA((2, NY - 1)),
@@ -812,10 +866,18 @@
             sds((7, CH, CH), F32), sds((CH, CH), F32), sds((CH, CW), F32), sds((9, CW, CW), F32),
             sds((CW, CW), F32),
         ),
-        in_specs=[VMEM, VMEM, anywhere, VMEM],
-        out_specs=(anywhere,) + (VMEM,) * 6,
-        scratch_shapes=[pltpu.SemaphoreType.DMA((8,))],
-        compiler_params=pltpu.CompilerParams(vmem_limit_bytes=32 * 2**20),
+        in_specs=[anywhere, VMEM, anywhere, anywhere],
+        out_specs=(anywhere,) * 2 + (VMEM,) * 3 + (anywhere,) * 2,
+        scratch_shapes=[
+            pltpu.VMEM((PAYLOAD + LATE, 128), BF16),
+            pltpu.VMEM((10, CW, CW), F32),
+            pltpu.VMEM((BD, CH, VOX), BF16),
+            pltpu.VMEM((128, CW), BF16),
+            pltpu.SemaphoreType.DMA((2, 9)),
+            pltpu.SemaphoreType.DMA((13,)),
+            pltpu.SemaphoreType.DMA((10,)),
+        ],
+        compiler_params=pltpu.CompilerParams(vmem_limit_bytes=62 * 2**20),
         name="results",
     )(summed, basis, fine_act, coarse_out)
     return (outs[0], outs[1].reshape(16, 8, CW)) + tuple(outs[2:])

time: 104 us -> 104 us (level)
  local copies, waits for them, and re-layouts: 4.48 us -> 0 us
  Pallas kernels: 97.7 us -> 102 us
    unnamed x8 -> x0, local copies, waits for them, and re-layouts: 4.48 us -> none
    pallas_call x1, Pallas kernels: 3.68 us -> 7.16 us  [shards(): pl.pallas_call(result_kernel, out_shape=(sds((BD, CH, VOX), BF16), sds((1...]
    pallas_call x1, Pallas kernels: 92.2 us -> 93.3 us  [shards(): pl.pallas_call(step_kernel, out_shape=(sds((BD, CH, VOX), BF16), sds((128...]
where the time goes in v4:
time: 104 us
  Pallas kernels  102 us (98%)
  between operations  1.29 us (1%)
    pallas_call x1, Pallas kernels, shards(): pl.pallas_call(step_kernel, out_shape=(sds((BD, CH, VOX), BF16), sds((128...  93.3 us
    pallas_call x1, Pallas kernels, shards(): pl.pallas_call(result_kernel, out_shape=(sds((BD, CH, VOX), BF16), sds((1...  7.16 us

profile of v4, /device:TPU:1, one launch (start us, length us, event | category | flops | bytes accessed | tf_op | source)
XLA Modules:
  0.0 104.2 jit_solution(7268662783829599738)
XLA Ops:
  1.3 0.6 maximum_bitcast_fusion.basis_ref
  1.9 1.9 %routes.1 = (s32[6,64]{1,0:T(8,128)}, s32[24,6]{1,0:T(8,128)}, s32[1,128]{1,0:T(1,128)}, f32[1,128]{1,0:T(1,128)}) custom-call(s32[6,64]{1,0:T(8,128)} %bitcast.11, s32[1,64]{1,0:T(1,128)} %bitcast.12, s32[1,64]{1,0:T(1,128)} %bitcast.13), custom_call_target="tpu_custom_call" | custom-call | tf_op jit(solution)/shard_map/routes/pallas_call | solution.py:772
  3.8 93.3 %step.1 = (bf16[64,64,512]{2,1,0:T(8,128)(2,1)}, bf16[128,256]{1,0:T(8,128)(2,1)}, bf16[6656,128]{1,0:T(8,128)(2,1)}) custom-call(s32[24,6]{1,0:T(8,128)} %get-tuple-element.21.src_ref, s32[6,64]{1,0:T(8,128)} %get-tuple-element.22.idx_ref, bf16[64,64,512]{2,1,0:T(8,128)(2,1)} %x_ref.1, bf16[9,256,256]{2,1,0:T(8,128)(2,1)} %ck_any.1, ...), custom_call_target="tpu_custom_call" | custom-call | tf_op jit(solution)/shard_map/step/pallas_call | solution.py:783
  97.1 7.2 %results.1 = (bf16[64,64,512]{2,1,0:T(8,128)(2,1)}, bf16[128,256]{1,0:T(8,128)(2,1)}, f32[7,64,64]{2,1,0:T(8,128)}, f32[64,64]{1,0:T(8,128)}, f32[64,256]{1,0:T(...) custom-call(bf16[6656,128]{1,0:T(8,128)(2,1)} %get-tuple-element.25.f_any, f32[1,64]{1,0:T(1,128)} %maximum_bitcast_fusion.basis_ref, ...), custom_call_target="tpu_custom_call" | custom-call | tf_op jit(solution)/shard_map/results/pallas_call | solution.py:862
  (1 shorter events, 0.0 us)
